TPU v7x, 256 devices: a whole 4x4x8 slice. The times are simulated.
256 devices in a mesh: replica: 16 (over x, z_hi), fsdp: 16 (over z_lo, y, core).
Axes of the slice: x: 4, y: 4, z: 8 (z_hi: 4, z_lo: 2; z = z_hi * 2 + z_lo), core: 2. Of those that a mesh axis runs over, the one named last changes fastest.
Arguments:
- tokens: bfloat16 [16, 8192, 4096], P('replica', 'fsdp'), may hold values from -6 to 6
- kv_cotangent: bfloat16 [16, 8192, 1024], P('replica', 'fsdp'), may hold values from -6 to 6
- inner_weights: bfloat16 [16, 4096, 1024], P('replica', 'fsdp'), may hold values from -0.125 to 0.125
- outer_params: float32 [4096, 1024], P('fsdp', 'replica'), may hold values from -0.09375 to 0.09375
- outer_momentum: float32 [4096, 1024], P('fsdp', 'replica'), may hold values from -0.12 to 0.12
Outputs:
- keys_values: bfloat16 [16, 8192, 1024], P('replica', 'fsdp')
- token_grads: bfloat16 [16, 8192, 4096], P('replica', 'fsdp')
- weight_grads: float32 [16, 4096, 1024], P('replica', 'fsdp')
- new_outer: float32 [4096, 1024], P('fsdp', 'replica')
- new_momentum: float32 [4096, 1024], P('fsdp', 'replica')
- synced_weights: bfloat16 [4096, 1024], P('fsdp')
All inputs are finite; a program needn't handle non-finite values.
Results may differ from a plain program's by a relative error of at most 0.013.
Values may be sent and summed in bfloat16 or wider, within the bound.
No kernel may reach another device: no remote copies, remote signals or barrier semaphores. Data moves between devices by JAX's collectives and lax.ppermute only.
A program may use at most 128 MiB of HBM per device.

v0:
```python
import jax
import jax.numpy as jnp
from jax import lax
from jax.sharding import PartitionSpec as P


def nesterov(params_in, moment_in, summed, replicas):
    pseudo = params_in - summed / replicas
    moment_out = 0.9 * moment_in + pseudo
    params_out = params_in - 0.7 * (pseudo + 0.9 * moment_out)
    return (params_out, moment_out)


def on_device(tokens, kv_cotangent, inner_weights, outer_params, outer_momentum):
    tok_rows = tokens[0]
    cot_rows = kv_cotangent[0]
    w_shard = inner_weights[0]
    replicas = lax.axis_size("replica")
    summed = lax.psum(w_shard.astype(jnp.float32).astype(jnp.bfloat16), "replica").astype(
        jnp.float32
    )
    whole_params, whole_moment = (
        lax.all_gather(outer_params, "replica", axis=1, tiled=True),
        lax.all_gather(outer_momentum, "replica", axis=1, tiled=True),
    )
    wide_outer, wide_moment = nesterov(whole_params, whole_moment, summed, replicas)
    synced_weights = wide_outer.astype(jnp.bfloat16)
    columns = outer_params.shape[1]
    offset = lax.axis_index("replica") * columns
    new_outer = lax.dynamic_slice_in_dim(wide_outer, offset, columns, 1)
    new_momentum = lax.dynamic_slice_in_dim(wide_moment, offset, columns, 1)
    whole_w = lax.all_gather(w_shard, "fsdp", axis=0, tiled=True)
    values = jnp.dot(tok_rows, whole_w, preferred_element_type=jnp.float32)
    back = lax.dot_general(
        cot_rows, whole_w, (((1,), (1,)), ((), ())), preferred_element_type=jnp.float32
    )
    grads = lax.psum_scatter(
        lax.dot_general(
            tok_rows, cot_rows, (((0,), (0,)), ((), ())), preferred_element_type=jnp.float32
        ),
        "fsdp",
        scatter_dimension=0,
        tiled=True,
    )
    keys_values = values.astype(jnp.bfloat16)[None]
    token_grads = back.astype(jnp.bfloat16)[None]
    return (keys_values, token_grads, grads[None], new_outer, new_momentum, synced_weights)


def solution(mesh):
    return jax.shard_map(
        on_device,
        mesh=mesh,
        in_specs=(
            P("replica", "fsdp", None),
            P("replica", "fsdp", None),
            P("replica", "fsdp", None),
            P("fsdp", "replica"),
            P("fsdp", "replica"),
        ),
        out_specs=(
            P("replica", "fsdp", None),
            P("replica", "fsdp", None),
            P("replica", "fsdp", None),
            P("fsdp", "replica"),
            P("fsdp", "replica"),
            P("fsdp", None),
        ),
        check_vma=False,
    )
```

profile of v0, /device:TPU:32, one launch (start us, length us, event | category | flops | bytes accessed | tf_op | source)
XLA Modules:
  0.0 452.3 jit_solution(14357951320860078112)
XLA Ops:
  7.2 0.0 copy-start
  7.2 0.0 all-reduce.2.cloned.1.call-start
  7.2 2.1 copy.15
  9.3 0.0 all-reduce.2.cloned.1.call-update
  9.4 0.0 all-gather.5.cloned.1.call-start
  9.4 0.7 all-gather.5.cloned.1.call-update
  10.1 0.0 all-gather.7.cloned.1.call-start
  10.2 0.7 all-gather.7.cloned.1.call-update
  10.9 0.0 all-gather.9.cloned.1.call-start
  10.9 0.5 all-gather.9.cloned.1.call-update
  11.4 0.0 reduce-scatter.2.cloned.1.call-start
  11.5 10.4 %fusion.10 = f32[4096,1024]{1,0:T(8,128)} fusion(bf16[1,512,4096]{2,1,0:T(8,128)(2,1)} %param.5, bf16[1,512,1024]{2,1,0:T(8,128)(2,1)S(1)} %copy-done), kind=kOutput, calls=%fused_computation.6 | convolution fusion | flops 4294967296 | bytes 22020096 | tf_op jit(solution)/shard_map/dot_general | solution.py:38
  21.9 0.0 reduce-scatter.2.cloned.1.call-update
  21.9 158.4 %all-reduce.2.cloned.1.call-done = bf16[256,1024]{0,1:T(8,128)(2,1)} async-done(((bf16[256,1024]{0,1:T(8,128)(2,1)}), bf16[256,1024]{0,1:T(8,128)(2,1)}) %all-reduce.2.cloned.1.call-update) | async-done | bytes 524304 | tf_op jit(solution)/shard_map/psum | solution.py:19
  180.3 52.4 %all-gather.5.cloned.1.call-done = f32[256,1024]{0,1:T(8,128)} async-done(((f32[256,64]{0,1:T(8,128)}), f32[256,1024]{0,1:T(8,128)}) %all-gather.5.cloned.1.call-update) | async-done | bytes 1048592 | tf_op jit(solution)/shard_map/all_gather | solution.py:23
  232.7 53.5 %all-gather.7.cloned.1.call-done = f32[256,1024]{0,1:T(8,128)} async-done(((f32[256,64]{0,1:T(8,128)}), f32[256,1024]{0,1:T(8,128)}) %all-gather.7.cloned.1.call-update) | async-done | bytes 1048592 | tf_op jit(solution)/shard_map/all_gather | solution.py:24
  286.2 3.0 fusion.25
  289.2 1.0 copy.16
  290.2 1.5 constant_dynamic-slice_fusion
  291.7 50.2 %all-gather.9.cloned.1.call-done = bf16[1,4096,1024]{2,1,0:T(8,128)(2,1)} async-done(((bf16[1,256,1024]{2,1,0:T(8,128)(2,1)}), bf16[1,4096,1024]{2,1,0:T(8,128)(2,1)}) %all-gather.9.cloned.1.call-update) | async-done | bytes 8388624 | tf_op jit(solution)/shard_map/all_gather | solution.py:32
  341.8 9.6 %fusion.7 = bf16[1,512,4096]{2,1,0:T(8,128)(2,1)} fusion(bf16[1,4096,1024]{2,1,0:T(8,128)(2,1)} %all-gather.9.cloned.1.call-done, bf16[1,512,1024]{2,1,0:T(8,128)(2,1)S(1)} %copy-done), kind=kOutput, calls=%fused_computation.5 | convolution fusion | flops 4297064448 | bytes 13631488 | tf_op jit(solution)/shard_map/dot_general | solution.py:34
  351.4 0.0 copy-done.2
  351.4 5.5 %fusion.18 = bf16[1,512,1024]{2,1,0:T(8,128)(2,1)} fusion(bf16[1,4096,1024]{2,1,0:T(8,128)(2,1)S(1)} %copy-done.1, bf16[1,512,4096]{2,1,0:T(8,128)(2,1)S(1)} %copy-done.2), kind=kOutput, calls=%fused_computation.10 | convolution fusion | flops 4295491584 | bytes 13631488 | tf_op jit(solution)/shard_map/dot_general | solution.py:33
  356.9 88.8 %reduce-scatter.2.cloned.1.call-done = f32[256,1024]{1,0:T(8,128)} async-done(((f32[4096,1024]{1,0:T(8,128)}), f32[256,1024]{1,0:T(8,128)}) %reduce-scatter.2.cloned.1.call-update) | async-done | bytes 1048592 | tf_op jit(solution)/shard_map/reduce_scatter | solution.py:37
  (4 shorter events, 0.0 us)
Async XLA Ops:
  7.2 4.3 copy-start
  7.2 173.1 %all-reduce.2.cloned.1.call-start = ((), (), s32[]{:S(2)}) async-start(), calls=%async_computation.3 | async-start | bytes 1048576 | tf_op jit(solution)/shard_map/psum | solution.py:19
  9.4 223.3 %all-gather.5.cloned.1.call-start = ((), (), s32[]{:S(2)}) async-start(), calls=%async_computation.2 | async-start | bytes 1114112 | tf_op jit(solution)/shard_map/all_gather | solution.py:23
  10.1 276.1 %all-gather.7.cloned.1.call-start = ((), (), s32[]{:S(2)}) async-start(), calls=%async_computation.4 | async-start | bytes 1114112 | tf_op jit(solution)/shard_map/all_gather | solution.py:24
  10.9 331.0 %all-gather.9.cloned.1.call-start = ((), (), s32[]{:S(2)}) async-start(), calls=%async_computation.5 | async-start | bytes 8912896 | tf_op jit(solution)/shard_map/all_gather | solution.py:32
  11.4 434.3 %reduce-scatter.2.cloned.1.call-start = ((), (), s32[]{:S(2)}) async-start(), calls=%async_computation.1 | async-start | bytes 17825792 | tf_op jit(solution)/shard_map/reduce_scatter | solution.py:37
  341.8 9.6 %copy-start.1 = (bf16[1,4096,1024]{2,1,0:T(8,128)(2,1)S(1)}, bf16[1,4096,1024]{2,1,0:T(8,128)(2,1)}, u32[]{:S(2)}) copy-start(bf16[1,4096,1024]{2,1,0:T(8,128)(2,1)} %all-gather.9.cloned.1.call-done) | copy-start | bytes 25165828
  341.8 9.6 %copy-start.2 = (bf16[1,512,4096]{2,1,0:T(8,128)(2,1)S(1)}, bf16[1,512,4096]{2,1,0:T(8,128)(2,1)}, u32[]{:S(2)}) copy-start(bf16[1,512,4096]{2,1,0:T(8,128)(2,1)} %param.5) | copy-start | bytes 12582916
Sparse Core Ops, SparseCore 0:
  11.2 169.0 all-reduce.1
  183.0 49.6 all-gather.4
  235.4 50.7 all-gather.6
  288.1 53.7 all-gather.8
  345.0 100.7 reduce-scatter.1
where the time goes:
time: 454 us; the launch traced here: 452 us
  waiting for transfers between devices  405 us (89%)
  matrix products  25.5 us (6%)
  between operations  13.8 us (3%)
  local copies, waits for them, and re-layouts  4.63 us (1%)
    psum x1, waiting for transfers between devices, on_device(): lax.psum(w_shard.astype(jnp.float32).astype(jnp.bfloat16), 'replica')  158 us
    reduce_scatter x1, waiting for transfers between devices, on_device(): lax.psum_scatter(lax.dot_general(tok_rows, cot_rows, (((0,), (0,)), ((),...  88.8 us
    all_gather x1, waiting for transfers between devices, on_device(): lax.all_gather(outer_momentum, 'replica', axis=1, tiled=True)  53.5 us
    all_gather x1, waiting for transfers between devices, on_device(): lax.all_gather(outer_params, 'replica', axis=1, tiled=True)  52.4 us
    all_gather x1, waiting for transfers between devices, on_device(): whole_w = lax.all_gather(w_shard, 'fsdp', axis=0, tiled=True)  50.2 us
    dot_general x1, matrix products, on_device(): lax.dot_general(tok_rows, cot_rows, (((0,), (0,)), ((), ())), preferred_e...  10.4 us
    dot_general x1, matrix products, on_device(): lax.dot_general(cot_rows, whole_w, (((1,), (1,)), ((), ())), preferred_el...  9.6 us
  transfers between devices with their start and end apart: 5, of which 5 were waited for; matrix products, arithmetic and copies ran while one was open for 7% of the time, Pallas kernels for 0%

commit v1 on v0

v1 whole, which is shorter than its diff:
```python
import functools

import jax
import jax.numpy as jnp
from jax import lax
from jax.experimental import pallas as pl
from jax.experimental.pallas import tpu as pltpu
from jax.sharding import PartitionSpec as P

NZ, NY, NC = 2, 4, 2
NX, NH = 4, 4
F32, BF16 = jnp.float32, jnp.bfloat16
VMEM_LIMIT = 60 * 1024 * 1024


def shift_fsdp(a, dz=0, dy=0, dc=0):
    pairs = []
    for z in range(NZ):
        for y in range(NY):
            for c in range(NC):
                to = (((z + dz) % NZ) * NY + (y + dy) % NY) * NC + (c + dc) % NC
                pairs.append(((z * NY + y) * NC + c, to))
    return lax.ppermute(a, "fsdp", pairs)


ANY = pl.BlockSpec(memory_space=pl.ANY)
SMEM = pl.BlockSpec(memory_space=pltpu.SMEM)


def place(me):
    return me // (NC * NY), (me // NC) % NY, me % NC


def block_at(z, y, c):
    return (z * NY + y) * NC + c


def columns(ref, b, width=256):
    return ref.at[:, pl.ds(pl.multiple_of(b * width, width), width)]


GRAD_DIMS = (((0,), (0,)), ((), ()))


def far_gradients(here, tok, tok_rx, cot, cot_rx, after):
    rows, kv = cot.shape

    def y_of(i, here):
        step = jnp.where(i == 0, 2, jnp.where(i == 1, 1, jnp.where(i == 2, 3, 0)))
        return (place(here[0])[1] + step) % NY

    def own_block(i, here):
        z, _, core = place(here[0])
        return 0, block_at(1 - z, y_of(i, here), core)

    def body(here_ref, t_ref, tr_ref, c_ref, cr_ref, *rest):
        a_ref, b_ref, d_ref = rest[len(after) :]
        i = pl.program_id(0)
        acc = lax.dot_general(t_ref[...], c_ref[...], GRAD_DIMS, preferred_element_type=F32)
        acc += lax.dot_general(tr_ref[...], cr_ref[...], GRAD_DIMS, preferred_element_type=F32)
        acc = acc.astype(BF16)

        @pl.when(i == 0)
        def _():
            a_ref[...] = acc

        @pl.when((i == 1) | (i == 2))
        def _():
            b_ref[...] = acc

        @pl.when(i == 3)
        def _():
            d_ref[...] = acc

    return pl.pallas_call(
        body,
        grid_spec=pltpu.PrefetchScalarGridSpec(
            num_scalar_prefetch=1,
            grid=(NY,),
            in_specs=[
                pl.BlockSpec((rows, 256), own_block),
                pl.BlockSpec((rows, 256), own_block),
                pl.BlockSpec((rows, kv), lambda i, here: (0, 0)),
                pl.BlockSpec((rows, kv), lambda i, here: (0, 0)),
            ]
            + [ANY] * len(after),
            out_specs=[
                pl.BlockSpec((256, kv), lambda i, here: (0, 0)),
                pl.BlockSpec((256, kv), lambda i, here: (jnp.clip(i - 1, 0, 1), 0)),
                pl.BlockSpec((256, kv), lambda i, here: (0, 0)),
            ],
        ),
        out_shape=[jax.ShapeDtypeStruct((m * 256, kv), BF16) for m in (1, 2, 1)],
        compiler_params=pltpu.CompilerParams(vmem_limit_bytes=VMEM_LIMIT),
        name="far_gradients",
    )(here, tok, tok_rx, cot, cot_rx, *after)


def add_blocks(own, jobs, dtype, after=(), along=()):
    kv = own.shape[1]
    flat = [(own, k, m) for m, (k, _) in enumerate(jobs)]
    flat += [(a, k, m) for m, (_, others) in enumerate(jobs) for a, k in others]
    n_in = len(flat) + len(after) + len(along)

    def body(*refs):
        ins, outs = refs[: len(flat)], refs[n_in : n_in + len(jobs)]
        for m, o in enumerate(outs):
            acc = ins[m][...]
            for ref, (_, _, job) in zip(ins[len(jobs) :], flat[len(jobs) :]):
                if job == m:
                    acc = acc + ref[...].astype(F32)
            o[...] = acc.astype(dtype)

    def spec(k):
        return pl.BlockSpec((256, kv), lambda i: (k, 0))

    return pl.pallas_call(
        body,
        grid=(1,),
        in_specs=[spec(k) for _, k, _ in flat] + [ANY] * (len(after) + len(along)),
        out_specs=[spec(0) for _ in jobs] + [ANY] * len(along),
        out_shape=[jax.ShapeDtypeStruct((256, kv), dtype) for _ in jobs]
        + [jax.ShapeDtypeStruct(a.shape, a.dtype) for a in along],
        input_output_aliases={len(flat) + len(after) + k: len(jobs) + k for k in range(len(along))},
        compiler_params=pltpu.CompilerParams(vmem_limit_bytes=VMEM_LIMIT),
        name="add_blocks",
    )(*[a for a, _, _ in flat], *after, *along)


def project(here, tok, tok_rx, cot, cot_rx, pieces, steps, before=None, after=()):
    rows, d = tok.shape
    kv = cot.shape[1]
    far = before is not None
    n_w = len(pieces)
    deep = NY * 256

    def body(here_ref, t_ref, tx_ref, c_ref, cx_ref, *rest):
        w_refs, rest = rest[:n_w], rest[n_w:]
        if far:
            own_in, send_in = rest[:2]
            rest = rest[4 + len(after) :]
            own_ref, tg_ref, out_ref = rest[:3]
            w_v, t_v, tr_v, c_v, cr_v, g_v, own_v, send_v, out_v, sems = rest[3:]
        else:
            rest = rest[len(after) :]
            own_ref, tg_ref, out_ref, send_ref, grad_ref = rest[:5]
            w_v, t_v, tr_v, c_v, cr_v, g_v, own_v, send_v, out_v, grad_v, sems = rest[5:]
        z, y, core = place(here_ref[0])
        zz = 1 - z if far else z
        ys = [(y + step) % NY for step in steps]
        count = [0]

        def copy(src, dst):
            c = pltpu.make_async_copy(src, dst, sems.at[count[0]])
            count[0] += 1
            c.start()
            return c

        ready_c = copy(c_ref, c_v)
        ready_w = [copy(r, w_v.at[pl.ds(k * 256, 256)]) for k, r in enumerate(w_refs)]
        ready_t = [copy(columns(t_ref, block_at(zz, yy, core)), columns(t_v, k)) for k, yy in enumerate(ys)]
        ready_cr = copy(cx_ref, cr_v)
        ready_tr = [copy(columns(tx_ref, block_at(zz, yy, core)), columns(tr_v, k)) for k, yy in enumerate(ys)]
        if far:
            ready_own = copy(own_in, own_v)
            ready_send = copy(send_in, send_v)
        done = []
        trans = (((1,), (1,)), ((), ()))
        ready_c.wait()
        for k in range(NY):
            ready_w[k].wait()
            at = slice(k * 256, k * 256 + 256)
            g_v[:, at] = lax.dot_general(
                c_v[...], w_v[at, :], trans, preferred_element_type=F32
            ).astype(BF16)
            done.append(copy(columns(g_v, k), columns(tg_ref, block_at(zz, ys[k], core))))
        for c in ready_t:
            c.wait()
        sums = jnp.dot(t_v[...], w_v[...], preferred_element_type=F32)
        if far:
            ready_own.wait()
            sums += own_v[...]
        own_v[...] = sums
        done.append(copy(own_v, own_ref))
        ready_cr.wait()
        out_v[:, :deep] = lax.dot_general(
            cr_v[...], w_v[...], trans, preferred_element_type=F32
        ).astype(BF16)
        for c in ready_tr:
            c.wait()
        sums = jnp.dot(tr_v[...], w_v[...], preferred_element_type=F32)
        if far:
            ready_send.wait()
            out_v[:, deep:] = (send_v[...] + sums).astype(BF16)
            done.append(copy(out_v, out_ref.at[:, pl.ds(deep, deep + kv)]))
        else:
            done.append(copy(out_v, out_ref.at[:, pl.ds(0, deep)]))
            send_v[...] = sums
            done.append(copy(send_v, send_ref))
            for k in range(NY):
                at = slice(k * 256, k * 256 + 256)
                acc = lax.dot_general(t_v[:, at], c_v[...], GRAD_DIMS, preferred_element_type=F32)
                acc += lax.dot_general(tr_v[:, at], cr_v[...], GRAD_DIMS, preferred_element_type=F32)
                grad_v[at, :] = acc
                done.append(copy(grad_v.at[pl.ds(k * 256, 256)], grad_ref.at[pl.ds(k * 256, 256)]))
        for c in done:
            c.wait()

    sums = jax.ShapeDtypeStruct((rows, kv), F32)
    out_shape = [
        sums,
        jax.ShapeDtypeStruct((rows, d), BF16),
        jax.ShapeDtypeStruct((rows, 2 * deep + kv), BF16),
    ]
    args = [here, tok, tok_rx, cot, cot_rx, *pieces]
    alias = {}
    scratch = [
        pltpu.VMEM((deep, kv), BF16),
        pltpu.VMEM((rows, deep), BF16),
        pltpu.VMEM((rows, deep), BF16),
        pltpu.VMEM((rows, kv), BF16),
        pltpu.VMEM((rows, kv), BF16),
        pltpu.VMEM((rows, deep), BF16),
        pltpu.VMEM((rows, kv), F32),
        pltpu.VMEM((rows, kv), F32),
        pltpu.VMEM((rows, deep + (kv if far else 0)), BF16),
    ]
    if far:
        own, send, grads_in, out_in = before
        alias = {len(args) + 2: 1, len(args) + 3: 2}
        args += [own, send, grads_in, out_in]
    else:
        gradient = jax.ShapeDtypeStruct((deep, kv), F32)
        out_shape += [sums, gradient]
        scratch.append(pltpu.VMEM(gradient.shape, F32))
    args += list(after)
    return pl.pallas_call(
        body,
        in_specs=[SMEM] + [ANY] * (len(args) - 1),
        out_specs=[ANY] * len(out_shape),
        out_shape=out_shape,
        scratch_shapes=scratch + [pltpu.SemaphoreType.DMA((32,))],
        input_output_aliases=alias,
        compiler_params=pltpu.CompilerParams(vmem_limit_bytes=VMEM_LIMIT),
        name="project",
    )(*args)


def merge(here, own, other_rx, grads, steps, after):
    rows, kv = own.shape
    deep = NY * 256

    def body(here_ref, own_ref, a_ref, _, *rest):
        kv_ref, tg_ref, own_v, a_v, kv_v, sems = rest[len(after) :]
        z, y, core = place(here_ref[0])
        count = [0]

        def copy(src, dst):
            c = pltpu.make_async_copy(src, dst, sems.at[count[0]])
            count[0] += 1
            c.start()
            return c

        load_kv = copy(a_ref.at[:, pl.ds(2 * deep, kv)], a_v.at[:, pl.ds(2 * deep, kv)])
        load_own = copy(own_ref, own_v)
        loads = [copy(columns(a_ref, k), columns(a_v, k)) for k in range(2 * NY)]
        out = []
        for k, load in enumerate(loads):
            load.wait()
            zz = z if k < NY else 1 - z
            at = block_at(zz, (y + steps[k % NY]) % NY, 1 - core)
            out.append(copy(columns(a_v, k), columns(tg_ref, at)))
        load_kv.wait()
        load_own.wait()
        kv_v[...] = (own_v[...] + a_v[:, 2 * deep :].astype(F32)).astype(BF16)
        out.append(copy(kv_v, kv_ref))
        for c in out:
            c.wait()

    return pl.pallas_call(
        body,
        in_specs=[SMEM] + [ANY] * (3 + len(after)),
        out_specs=[ANY, ANY],
        out_shape=[
            jax.ShapeDtypeStruct((rows, kv), BF16),
            jax.ShapeDtypeStruct(grads.shape, BF16),
        ],
        scratch_shapes=[
            pltpu.VMEM((rows, kv), F32),
            pltpu.VMEM(other_rx.shape, BF16),
            pltpu.VMEM((rows, kv), BF16),
            pltpu.SemaphoreType.DMA((4 * NY + 3,)),
        ],
        input_output_aliases={3: 1},
        compiler_params=pltpu.CompilerParams(vmem_limit_bytes=VMEM_LIMIT),
        name="merge",
    )(here, own, other_rx, grads, *after)


WHOLE = pl.BlockSpec(memory_space=pltpu.VMEM)


def shift_replica(a, dx=0, dh=0):
    pairs = [
        (x * NH + h, ((x + dx) % NX) * NH + (h + dh) % NH) for x in range(NX) for h in range(NH)
    ]
    return lax.ppermute(a, "replica", pairs)


def small_call(body, n_in, after, out_shape, scratch, name):
    return pl.pallas_call(
        body,
        in_specs=[SMEM] + [WHOLE] * n_in + [ANY] * len(after),
        out_specs=[WHOLE] * len(out_shape),
        out_shape=out_shape,
        scratch_shapes=scratch,
        compiler_params=pltpu.CompilerParams(vmem_limit_bytes=VMEM_LIMIT),
        name=name,
    )


X_GROUPS = [[x * NH + h for x in range(NX)] for h in range(NH)]
H_GROUPS = [[x * NH + h for h in range(NH)] for x in range(NX)]


def sum_along_x(here, parts, after):
    _, rows, wide = parts.shape
    thin = wide // NH

    def body(here_ref, p_ref, *rest):
        out_ref = rest[len(after)]
        acc = p_ref[0].astype(F32)
        for k in range(1, NX):
            acc += p_ref[k].astype(F32)
        out_ref[...] = acc.T.astype(BF16).reshape(NH, thin, rows)

    out = [jax.ShapeDtypeStruct((NH, thin, rows), BF16)]
    return small_call(body, 1, after, out, [], "sum_along_x")(here, parts, *after)[0]


def outer_step(here, parts, params, moment, after):
    def body(here_ref, t_ref, p_ref, m_ref, *rest):
        np_ref, nm_ref, s_ref = rest[len(after) :]
        total = t_ref[0].astype(F32)
        for k in range(1, NH):
            total += t_ref[k].astype(F32)
        p = p_ref[...]
        pseudo = p - total / (NX * NH)
        nm = 0.9 * m_ref[...] + pseudo
        new = p - 0.7 * (pseudo + 0.9 * nm)
        nm_ref[...] = nm
        np_ref[...] = new
        s_ref[...] = new.astype(BF16)

    out = [jax.ShapeDtypeStruct(params.shape, d) for d in (F32, F32, BF16)]
    return small_call(body, 3, after, out, [], "outer_step")(here, parts, params, moment, *after)


def join_h(here, parts, after):
    thin, rows = parts[0].shape

    def body(here_ref, *rest):
        part_refs, out_ref, total = rest[:NH], rest[-2], rest[-1]
        h = here_ref[1] % NH
        for k in range(NH):
            at = pl.multiple_of(((h + NH - k) % NH) * thin, thin)
            total[pl.ds(at, thin), :] = part_refs[k][...].astype(F32)
        out_ref[...] = total[...].T.astype(BF16)

    return small_call(
        body,
        NH,
        after,
        [jax.ShapeDtypeStruct((rows, NH * thin), BF16)],
        [pltpu.VMEM((NH * thin, rows), F32)],
        "join_h",
    )(here, *parts, *after)[0]


def join_x(here, parts, after):
    rows, wide = parts[0].shape

    def body(here_ref, *rest):
        part_refs, out_ref, sems = rest[:NX], rest[-2], rest[-1]
        x = here_ref[1] // NH
        copies = [
            pltpu.make_async_copy(
                part_refs[k], columns(out_ref, (x + NX - k) % NX, wide), sems.at[k]
            )
            for k in range(NX)
        ]
        for c in copies:
            c.start()
        for c in copies:
            c.wait()

    return pl.pallas_call(
        body,
        in_specs=[SMEM] + [WHOLE] * NX + [ANY] * len(after),
        out_specs=ANY,
        out_shape=jax.ShapeDtypeStruct((rows, NX * wide), BF16),
        scratch_shapes=[pltpu.SemaphoreType.DMA((NX,))],
        compiler_params=pltpu.CompilerParams(vmem_limit_bytes=VMEM_LIMIT),
        name="join_x",
    )(here, *parts, *after)


def on_device(tokens, kv_cotangent, inner_weights, outer_params, outer_momentum):
    tok, cot, w = tokens[0], kv_cotangent[0], inner_weights[0]
    here = jnp.stack([lax.axis_index(a).astype(jnp.int32) for a in ("fsdp", "replica")])

    w_dn = shift_fsdp(w, dy=1)
    w_up = shift_fsdp(w, dy=-1)
    w_z = shift_fsdp(w, dz=1)

    tok_rx = shift_fsdp(tok, dc=1)
    cot_rx = shift_fsdp(cot, dc=1)

    parts = w.reshape(w.shape[0], NX, w.shape[1] // NX).transpose(1, 0, 2)
    parts = lax.all_to_all(parts, "replica", 0, 0, axis_index_groups=X_GROUPS, tiled=True)
    sum_x = sum_along_x(here, parts, ())

    w_op = shift_fsdp(w_dn, dy=1)
    wz_up = shift_fsdp(w_z, dy=-1)
    wz_dn = shift_fsdp(w_z, dy=1)
    wz_op = shift_fsdp(wz_up, dy=-1)

    g1, g2, g3 = far_gradients(here, tok, tok_rx, cot, cot_rx, (sum_x, w_dn, w_up, w_z))
    r1 = shift_fsdp(g1, dz=1)
    r2 = shift_fsdp(g2, dz=1)
    r3 = shift_fsdp(g3, dz=1)

    steps = (0, NY - 1, 1, 2)
    kv_own, grads, to_core, kv_send, own = project(
        here, tok, tok_rx, cot, cot_rx, [w, w_dn, w_up, w_op], steps, after=(g1,)
    )

    to_up, sum_x = add_blocks(own, [(3, [(r1, 0)])], BF16, along=(sum_x,))
    total = lax.all_to_all(sum_x, "replica", 0, 0, axis_index_groups=H_GROUPS, tiled=True)
    two_down = shift_fsdp(to_up, dy=1)

    to_up, to_dn = add_blocks(
        own, [(2, [(r2, 0), (two_down, 0)]), (1, [(r2, 1)])], BF16, ()
    )
    from_dn = shift_fsdp(to_up, dy=1)
    from_up = shift_fsdp(to_dn, dy=-1)

    new_params, new_moment, synced = outer_step(
        here, total, outer_params.T, outer_momentum.T, (to_up,)
    )
    synced = [synced] + [shift_replica(synced, dh=k) for k in range(1, NH)]
    kv_own, grads, to_core = project(
        here,
        tok,
        tok_rx,
        cot,
        cot_rx,
        [w_z, wz_dn, wz_up, wz_op],
        steps,
        (kv_own, kv_send, grads, to_core),
        after=(synced[0],),
    )
    other_rx = shift_fsdp(to_core, dc=1)
    keys_values, token_grads = merge(here, kv_own, other_rx, grads, steps, (kv_own,))
    synced = join_h(here, synced, (keys_values,))
    synced = [synced] + [shift_replica(synced, dx=k) for k in range(1, NX)]
    (weight_grads,) = add_blocks(
        own, [(0, [(r3, 0), (from_dn, 0), (from_up, 0)])], F32, (synced[0],)
    )
    synced = join_x(here, synced, (weight_grads,))

    return (
        keys_values[None],
        token_grads[None],
        weight_grads[None],
        new_params.T,
        new_moment.T,
        synced,
    )


def solution(mesh):
    return jax.shard_map(
        on_device,
        mesh=mesh,
        in_specs=(
            P("replica", "fsdp", None),
            P("replica", "fsdp", None),
            P("replica", "fsdp", None),
            P("fsdp", "replica"),
            P("fsdp", "replica"),
        ),
        out_specs=(
            P("replica", "fsdp", None),
            P("replica", "fsdp", None),
            P("replica", "fsdp", None),
            P("fsdp", "replica"),
            P("fsdp", "replica"),
            P("fsdp", None),
        ),
        check_vma=False,
    )
```

time: 454 us -> 134 us (0.30)
  waiting for transfers between devices: 405 us -> 28.6 us
  Pallas kernels: 0 us -> 50 us
  starting transfers between devices: 0.19 us -> 40.4 us
  matrix products: 25.5 us -> 0 us
  between operations: 13.8 us -> 1.08 us
  local copies, waits for them, and re-layouts: 4.63 us -> 12.2 us
    psum x1 -> x0, waiting for transfers between devices: 158 us -> none  [on_device(): lax.psum(w_shard.astype(jnp.float32).astype(jnp.bfloat16), 'replica')]
    all_gather x3 -> x0, waiting for transfers between devices: 156 us -> none  [the longest x1 53.5 us: on_device(): lax.all_gather(outer_momentum, 'replica', axis=1, tiled=True)]
    reduce_scatter x1 -> x0, waiting for transfers between devices: 88.8 us -> none  [on_device(): lax.psum_scatter(lax.dot_general(tok_rows, cot_rows, (((0,), (0,)), ((),...]
    pallas_call x0 -> x11, Pallas kernels: none -> 50 us  [the longest x2 23.1 us: project(): pl.pallas_call(body, in_specs=[SMEM] + [ANY] * (len(args) - 1), out_specs...]
    ppermute x0 -> x22, starting transfers between devices: none -> 29.6 us  [the longest x16 18 us: shift_fsdp(): return lax.ppermute(a, 'fsdp', pairs)]
    dot_general x3 -> x0, matrix products: 25.5 us -> none  [the longest x1 10.4 us: on_device(): lax.dot_general(tok_rows, cot_rows, (((0,), (0,)), ((), ())), preferred_e...]
    ppermute x0 -> x22, waiting for transfers between devices: none -> 20.1 us  [the longest x6 14.5 us: shift_replica(): return lax.ppermute(a, 'replica', pairs)]
    all_to_all x0 -> x2, starting transfers between devices: none -> 10.8 us  [the longest x1 7.35 us: on_device(): lax.all_to_all(sum_x, 'replica', 0, 0, axis_index_groups=H_GROUPS, tiled=...]
  transfers between devices with their start and end apart: 5 -> 24, of which waited for: 5 -> 6; matrix products, arithmetic and copies ran while one was open for 7% -> 2% of each run, Pallas kernels for 0% -> 28%
where the time goes in v1:
time: 134 us; the launch traced here: 133 us
  Pallas kernels  50 us (37%)
  starting transfers between devices  40.4 us (30%)
  waiting for transfers between devices  28.6 us (21%)
  local copies, waits for them, and re-layouts  12.2 us (9%)
    pallas_call x2, Pallas kernels, project(): pl.pallas_call(body, in_specs=[SMEM] + [ANY] * (len(args) - 1), out_specs...  23.1 us
    ppermute x16, starting transfers between devices, shift_fsdp(): return lax.ppermute(a, 'fsdp', pairs)  18 us
    ppermute x6, waiting for transfers between devices, shift_replica(): return lax.ppermute(a, 'replica', pairs)  14.5 us
    ppermute x6, starting transfers between devices, shift_replica(): return lax.ppermute(a, 'replica', pairs)  11.6 us
    unnamed x45, local copies, waits for them, and re-layouts  11.2 us
    all_to_all x1, waiting for transfers between devices, on_device(): lax.all_to_all(parts, 'replica', 0, 0, axis_index_groups=X_GROUPS, tiled=...  8.51 us
    pallas_call x3, Pallas kernels, add_blocks(): pl.pallas_call(body, grid=(1,), in_specs=[spec(k) for _, k, _ in flat] +...  8.2 us
    all_to_all x1, starting transfers between devices, on_device(): lax.all_to_all(sum_x, 'replica', 0, 0, axis_index_groups=H_GROUPS, tiled=...  7.35 us
  transfers between devices with their start and end apart: 24, of which 6 were waited for; matrix products, arithmetic and copies ran while one was open for 2% of the time, Pallas kernels for 28%

profile of v1, /device:TPU:32, one launch (start us, length us, event | category | flops | bytes accessed | tf_op | source)
XLA Modules:
  0.0 133.0 jit_solution(7136579670799628482)
XLA Ops:
  2.8 1.7 %collective-permute-start.7 = (bf16[256,1024]{1,0:T(8,128)(2,1)}, bf16[256,1024]{1,0:T(8,128)(2,1)S(1)}, u32[]{:S(2)}, u32[]{:S(2)}) collective-permute-start(bf16[256,1024]{1,0:T(8,128)(2,1)} %bitcast.25), channel_id=1, source_target_pairs={{0,6},{1,7},{2,0},{3,1},{4,2},{5,3},{6,4},{7,5},{8,14},{9,15},{10,... | collective-permute-start | bytes 1572872 | tf_op jit(solution)/shard_map/ppermute | solution.py:23
  4.5 1.8 %collective-permute-start.2 = (bf16[256,1024]{1,0:T(8,128)(2,1)}, bf16[256,1024]{1,0:T(8,128)(2,1)S(1)}, u32[]{:S(2)}, u32[]{:S(2)}) collective-permute-start(bf16[256,1024]{1,0:T(8,128)(2,1)} %bitcast.26), channel_id=1, source_target_pairs={{0,8},{1,9},{2,10},{3,11},{4,12},{5,13},{6,14},{7,15},{8,0},{9,1},... | collective-permute-start | bytes 1572872 | tf_op jit(solution)/shard_map/ppermute | solution.py:23
  8.6 3.5 %all-to-all-start = ((bf16[4,256,256]{2,1,0:T(8,128)(2,1)}), bf16[4,256,256]{2,1,0:T(8,128)(2,1)S(1)}, u32[]{:S(2)}, u32[]{:S(2)}) async-start(bf16[4,256,256]{2,1,0:T(8,128)(2,1)} %bitcast.6), calls=%async_computation | async-start | bytes 1048576 | tf_op jit(solution)/shard_map/all_to_all | solution.py:420
  12.7 8.5 %all-to-all-done.p_ref = bf16[4,256,256]{2,1,0:T(8,128)(2,1)S(1)} async-done(((bf16[4,256,256]{2,1,0:T(8,128)(2,1)}), bf16[4,256,256]{2,1,0:T(8,128)(2,1)S(1)}, u32[]{:S(2)}, u32[]{:S(2)}) %all-to-all-start) | async-done | bytes 524320 | tf_op jit(solution)/shard_map/all_to_all | solution.py:420
  22.0 1.8 %sum_along_x.1.rest_0_.refs_2_ = bf16[4,64,256]{2,1,0:T(8,128)(2,1)} custom-call(s32[2]{0:T(128)} %pad_add_fusion.here_ref, bf16[4,256,256]{2,1,0:T(8,128)(2,1)} %copy-done.5), custom_call_target="tpu_custom_call" | custom-call | tf_op jit(solution)/shard_map/sum_along_x/pallas_call | solution.py:338
  25.3 7.3 %far_gradients.1 = (bf16[256,1024]{1,0:T(8,128)(2,1)}, bf16[512,1024]{1,0:T(8,128)(2,1)}, bf16[256,1024]{1,0:T(8,128)(2,1)}) custom-call(s32[2]{0:T(128)} %pad_add_fusion.here_ref, bf16[512,4096]{1,0:T(8,128)(2,1)} %bitcast.15, bf16[512,4096]{1,0:T(8,128)(2,1)} %collective-permute-done.tr_ref.tx_ref, bf16[512,1024]{1,0:T(8,128)(2,1)} %bitcast.20, ...), custom_call_target="tpu_custom_call" | custom-call | tf_op jit(solution)/shard_map/far_gradients/pallas_call | solution.py:75
  34.6 3.1 %collective-permute-start.4 = (bf16[256,1024]{1,0:T(8,128)(2,1)}, bf16[256,1024]{1,0:T(8,128)(2,1)S(1)}, u32[]{:S(2)}, u32[]{:S(2)}) collective-permute-start(bf16[256,1024]{1,0:T(8,128)(2,1)} %copy-done.6), channel_id=1, source_target_pairs={{0,6},{1,7},{2,0},{3,1},{4,2},{5,3},{6,4},{7,5},{8,14},{9,15},{10,... | collective-permute-start | bytes 1572872 | tf_op jit(solution)/shard_map/ppermute | solution.py:23
  38.5 12.1 %project.2 = (f32[512,1024]{1,0:T(8,128)}, bf16[512,4096]{1,0:T(8,128)(2,1)}, bf16[512,3072]{1,0:T(8,128)(2,1)}, f32[512,1024]{1,0:T(8,128)}, f32[1024,1024]{1,0:T(8,128)}) custom-call(s32[2]{0:T(128)} %pad_add_fusion.here_ref, bf16[512,4096]{1,0:T(8,128)(2,1)} %bitcast.16, bf16[512,4096]{1,0:T(8,128)(2,1)} %collective-permute-done.tr_ref.tx_ref, ...), custom_call_target="tpu_custom_call" | custom-call | tf_op jit(solution)/shard_map/project/pallas_call | solution.py:237
  51.5 2.2 %add_blocks.3 = (bf16[256,1024]{1,0:T(8,128)(2,1)}, bf16[4,64,256]{2,1,0:T(8,128)(2,1)}) custom-call(f32[1024,1024]{1,0:T(8,128)} %get-tuple-element.31.refs_0_.refs_1_, bf16[256,1024]{1,0:T(8,128)(2,1)} %copy-done.9, bf16[4,64,256]{2,1,0:T(8,128)(2,1)} %sum_along_x.1.rest_0_.refs_2_), custom_call_target="tpu_custom_call", output_to_operand_aliasing={{1}: (2, {})} | custom-call | tf_op jit(solution)/shard_map/add_blocks/pallas_call | solution.py:117
  53.8 3.3 %collective-permute-start.5 = (bf16[256,1024]{1,0:T(8,128)(2,1)S(1)}, bf16[256,1024]{1,0:T(8,128)(2,1)}, u32[]{:S(2)}, u32[]{:S(2)}) collective-permute-start(bf16[256,1024]{1,0:T(8,128)(2,1)S(1)} %collective-permute-done.4.rest_2_), channel_id=1, source_target_pairs={{0,6},{1,7},{2,0},{3,1},{4,2},{5,3},{6,4},{7,5},{8,14},{9,15},{10,... | collective-permute-start | bytes 1572872 | tf_op jit(solution)/shard_map/ppermute | solution.py:23
  57.1 7.4 %all-to-all-start.1 = ((bf16[4,64,256]{2,1,0:T(8,128)(2,1)}), bf16[4,64,256]{2,1,0:T(8,128)(2,1)S(1)}, u32[]{:S(2)}, u32[]{:S(2)}) async-start(bf16[4,64,256]{2,1,0:T(8,128)(2,1)} %get-tuple-element.32), calls=%async_computation.1 | async-start | bytes 262144 | tf_op jit(solution)/shard_map/all_to_all | solution.py:439
  64.4 5.6 %collective-permute-done.11.refs_3_ = bf16[256,1024]{1,0:T(8,128)(2,1)S(1)} collective-permute-done((bf16[256,1024]{1,0:T(8,128)(2,1)}, bf16[256,1024]{1,0:T(8,128)(2,1)S(1)}, u32[]{:S(2)}, u32[]{:S(2)}) %collective-permute-start.11) | collective-permute-done | bytes 524320 | tf_op jit(solution)/shard_map/ppermute | solution.py:23
  71.8 3.1 %add_blocks.4 = (bf16[256,1024]{1,0:T(8,128)(2,1)}, bf16[256,1024]{1,0:T(8,128)(2,1)}) custom-call(f32[1024,1024]{1,0:T(8,128)} %get-tuple-element.31.refs_0_.refs_1_, f32[1024,1024]{1,0:T(8,128)} %get-tuple-element.31.refs_0_.refs_1_, bf16[512,1024]{1,0:T(8,128)(2,1)} %copy-done.1, bf16[256,1024]{1,0:T(8,128)(2,1)} %copy-done.12, bf16[512,1024]{1,0:T(8,128)(2,1)} %copy-done.1), custom_call_target="tpu_custom_call" | custom-call | tf_op jit(solution)/shard_map/add_blocks/pallas_call | solution.py:117
  75.6 1.6 %outer_step.1 = (f32[64,256]{1,0:T(8,128)}, f32[64,256]{1,0:T(8,128)}, bf16[64,256]{1,0:T(8,128)(2,1)}) custom-call(s32[2]{0:T(128)} %pad_add_fusion.here_ref, bf16[4,64,256]{2,1,0:T(8,128)(2,1)} %copy-done.11, f32[64,256]{1,0:T(8,128)} %bitcast.30, f32[64,256]{1,0:T(8,128)} %bitcast.31, bf16[256,1024]{1,0:T(8,128)(2,1)} %get-tuple-element.35.rest_0_), custom_call_target="tpu_custom_call" | custom-call | tf_op jit(solution)/shard_map/outer_step/pallas_call | solution.py:356
  78.0 10.9 %project.3 = (f32[512,1024]{1,0:T(8,128)}, bf16[512,4096]{1,0:T(8,128)(2,1)}, bf16[512,3072]{1,0:T(8,128)(2,1)}) custom-call(s32[2]{0:T(128)} %pad_add_fusion.here_ref, bf16[512,4096]{1,0:T(8,128)(2,1)} %bitcast.17, bf16[512,4096]{1,0:T(8,128)(2,1)} %collective-permute-done.tr_ref.tx_ref, ...), custom_call_target="tpu_custom_call", output_to_operand_aliasing={{1}: (11, {}), {2}: (12, {})} | custom-call | tf_op jit(solution)/shard_map/project/pallas_call | solution.py:237
  90.1 2.8 %collective-permute-start.15 = (bf16[256,1024]{1,0:T(8,128)(2,1)}, bf16[256,1024]{1,0:T(8,128)(2,1)}, u32[]{:S(2)}, u32[]{:S(2)}) collective-permute-start(bf16[256,1024]{1,0:T(8,128)(2,1)} %get-tuple-element.43), channel_id=1, source_target_pairs={{0,6},{1,7},{2,0},{3,1},{4,2},{5,3},{6,4},{7,5},{8,14},{9,15},{10,... | collective-permute-start | bytes 1572872 | tf_op jit(solution)/shard_map/ppermute | solution.py:23
  92.9 4.5 %collective-permute-start.18 = (bf16[64,256]{1,0:T(8,128)(2,1)S(1)}, bf16[64,256]{1,0:T(8,128)(2,1)S(1)}, u32[]{:S(2)}, u32[]{:S(2)}) collective-permute-start(bf16[64,256]{1,0:T(8,128)(2,1)S(1)} %copy-done.15), channel_id=1, source_target_pairs={{0,48},{16,0},{32,16},{48,32},{64,112},{80,64},{96,80},{112,96},{1... | collective-permute-start | bytes 98312 | tf_op jit(solution)/shard_map/ppermute | solution.py:307
  97.3 9.7 %collective-permute-done.18.rest_3_ = bf16[64,256]{1,0:T(8,128)(2,1)S(1)} collective-permute-done((bf16[64,256]{1,0:T(8,128)(2,1)S(1)}, bf16[64,256]{1,0:T(8,128)(2,1)S(1)}, u32[]{:S(2)}, u32[]{:S(2)}) %collective-permute-start.18) | collective-permute-done | bytes 32800 | tf_op jit(solution)/shard_map/ppermute | solution.py:307
  107.0 4.5 %collective-permute-start.17 = (bf16[64,256]{1,0:T(8,128)(2,1)S(1)}, bf16[64,256]{1,0:T(8,128)(2,1)S(1)}, u32[]{:S(2)}, u32[]{:S(2)}) collective-permute-start(bf16[64,256]{1,0:T(8,128)(2,1)S(1)} %copy-done.15), channel_id=1, source_target_pairs={{0,32},{16,48},{32,0},{48,16},{64,96},{80,112},{96,64},{112,80},{1... | collective-permute-start | bytes 98312 | tf_op jit(solution)/shard_map/ppermute | solution.py:307
  111.5 1.6 %copy-done.2 = bf16[512,3072]{1,0:T(8,128)(2,1)} copy-done((bf16[512,3072]{1,0:T(8,128)(2,1)}, bf16[512,3072]{1,0:T(8,128)(2,1)S(1)}, u32[]{:S(2)}) %copy-start.2) | copy-done | bytes 3145752
  113.2 4.5 %merge.1 = (bf16[512,1024]{1,0:T(8,128)(2,1)}, bf16[512,4096]{1,0:T(8,128)(2,1)}) custom-call(s32[2]{0:T(128)} %pad_add_fusion.here_ref, f32[512,1024]{1,0:T(8,128)} %get-tuple-element.37.own_ref.rest_0_, bf16[512,3072]{1,0:T(8,128)(2,1)} %copy-done.2, bf16[512,4096]{1,0:T(8,128)(2,1)} %get-tuple-element.39._, ...), custom_call_target="tpu_custom_call", output_to_operand_aliasing={{1}: (3, {})} | custom-call | tf_op jit(solution)/shard_map/merge/pallas_call | solution.py:280
  122.6 2.9 %add_blocks.5.rest_4_ = f32[256,1024]{1,0:T(8,128)} custom-call(f32[1024,1024]{1,0:T(8,128)} %get-tuple-element.31.refs_0_.refs_1_, bf16[256,1024]{1,0:T(8,128)(2,1)} %collective-permute-done.13.refs_1_, bf16[256,1024]{1,0:T(8,128)(2,1)} %collective-permute-done.14.refs_2_, bf16[256,1024]{1,0:T(8,128)(2,1)} %collective-permute-done.15.refs_3_, ...), custom_call_target="tpu_custom_call" | custom-call | tf_op jit(solution)/shard_map/add_blocks/pallas_call | solution.py:117
  126.4 2.4 %collective-permute-done.20.rest_2_ = bf16[256,256]{1,0:T(8,128)(2,1)S(1)} collective-permute-done((bf16[256,256]{1,0:T(8,128)(2,1)}, bf16[256,256]{1,0:T(8,128)(2,1)S(1)}, u32[]{:S(2)}, u32[]{:S(2)}) %collective-permute-start.20) | collective-permute-done | bytes 131104 | tf_op jit(solution)/shard_map/ppermute | solution.py:307
  130.8 1.9 %join_x.1 = bf16[256,1024]{1,0:T(8,128)(2,1)} custom-call(s32[2]{0:T(128)} %pad_add_fusion.here_ref, bf16[256,256]{1,0:T(8,128)(2,1)} %join_h.1.refs_4_.rest_0_, bf16[256,256]{1,0:T(8,128)(2,1)} %copy-done.18, bf16[256,256]{1,0:T(8,128)(2,1)} %copy-done.17, bf16[256,256]{1,0:T(8,128)(2,1)} %copy-done.16, f32[256,1024]{1,0:T(8,128)} %add_blocks.5.rest_4_), custom_call_target="tpu_custom_call" | custom-call | tf_op jit(solution)/shard_map/join_x/pallas_call | solution.py:397
  (82 shorter events, 23.1 us)
Async XLA Ops:
  0.6 23.3 %collective-permute-start = (bf16[512,4096]{1,0:T(8,128)(2,1)}, bf16[512,4096]{1,0:T(8,128)(2,1)}, u32[]{:S(2)}, u32[]{:S(2)}) collective-permute-start(bf16[512,4096]{1,0:T(8,128)(2,1)} %bitcast.14), channel_id=1, source_target_pairs={{0,1},{1,0},{2,3},{3,2},{4,5},{5,4},{6,7},{7,6},{8,9},{9,8},{10,11... | collective-permute-start | bytes 12582920 | tf_op jit(solution)/shard_map/ppermute | solution.py:23
  0.7 23.2 %collective-permute-start.1 = (bf16[512,1024]{1,0:T(8,128)(2,1)}, bf16[512,1024]{1,0:T(8,128)(2,1)S(1)}, u32[]{:S(2)}, u32[]{:S(2)}) collective-permute-start(bf16[512,1024]{1,0:T(8,128)(2,1)} %bitcast.19), channel_id=1, source_target_pairs={{0,1},{1,0},{2,3},{3,2},{4,5},{5,4},{6,7},{7,6},{8,9},{9,8},{10,11... | collective-permute-start | bytes 3145736 | tf_op jit(solution)/shard_map/ppermute | solution.py:23
  1.2 22.6 %collective-permute-start.6 = (bf16[256,1024]{1,0:T(8,128)(2,1)}, bf16[256,1024]{1,0:T(8,128)(2,1)S(1)}, u32[]{:S(2)}, u32[]{:S(2)}) collective-permute-start(bf16[256,1024]{1,0:T(8,128)(2,1)} %bitcast.24), channel_id=1, source_target_pairs={{0,2},{1,3},{2,4},{3,5},{4,6},{5,7},{6,0},{7,1},{8,10},{9,11},{10,... | collective-permute-start | bytes 1572872 | tf_op jit(solution)/shard_map/ppermute | solution.py:23
  2.8 21.1 %collective-permute-start.7 = (bf16[256,1024]{1,0:T(8,128)(2,1)}, bf16[256,1024]{1,0:T(8,128)(2,1)S(1)}, u32[]{:S(2)}, u32[]{:S(2)}) collective-permute-start(bf16[256,1024]{1,0:T(8,128)(2,1)} %bitcast.25), channel_id=1, source_target_pairs={{0,6},{1,7},{2,0},{3,1},{4,2},{5,3},{6,4},{7,5},{8,14},{9,15},{10,... | collective-permute-start | bytes 1572872 | tf_op jit(solution)/shard_map/ppermute | solution.py:23
  4.5 19.4 %collective-permute-start.2 = (bf16[256,1024]{1,0:T(8,128)(2,1)}, bf16[256,1024]{1,0:T(8,128)(2,1)S(1)}, u32[]{:S(2)}, u32[]{:S(2)}) collective-permute-start(bf16[256,1024]{1,0:T(8,128)(2,1)} %bitcast.26), channel_id=1, source_target_pairs={{0,8},{1,9},{2,10},{3,11},{4,12},{5,13},{6,14},{7,15},{8,0},{9,1},... | collective-permute-start | bytes 1572872 | tf_op jit(solution)/shard_map/ppermute | solution.py:23
  8.6 12.6 %all-to-all-start = ((bf16[4,256,256]{2,1,0:T(8,128)(2,1)}), bf16[4,256,256]{2,1,0:T(8,128)(2,1)S(1)}, u32[]{:S(2)}, u32[]{:S(2)}) async-start(bf16[4,256,256]{2,1,0:T(8,128)(2,1)} %bitcast.6), calls=%async_computation | async-start | bytes 1048576 | tf_op jit(solution)/shard_map/all_to_all | solution.py:420
  23.9 13.9 %collective-permute-start.8 = (bf16[256,1024]{1,0:T(8,128)(2,1)S(1)}, bf16[256,1024]{1,0:T(8,128)(2,1)S(1)}, u32[]{:S(2)}, u32[]{:S(2)}) collective-permute-start(bf16[256,1024]{1,0:T(8,128)(2,1)S(1)} %collective-permute-done.6.rest_1_), channel_id=1, source_target_pairs={{0,2},{1,3},{2,4},{3,5},{4,6},{5,7},{6,0},{7,1},{8,10},{9,11},{10,... | collective-permute-start | bytes 1572872 | tf_op jit(solution)/shard_map/ppermute | solution.py:23
  32.6 18.1 %collective-permute-start.9 = (bf16[256,1024]{1,0:T(8,128)(2,1)}, bf16[256,1024]{1,0:T(8,128)(2,1)S(1)}, u32[]{:S(2)}, u32[]{:S(2)}) collective-permute-start(bf16[256,1024]{1,0:T(8,128)(2,1)} %get-tuple-element.26.rest_4_), channel_id=1, source_target_pairs={{0,8},{1,9},{2,10},{3,11},{4,12},{5,13},{6,14},{7,15},{8,0},{9,1},... | collective-permute-start | bytes 1572872 | tf_op jit(solution)/shard_map/ppermute | solution.py:23
  33.6 36.4 %collective-permute-start.10 = (bf16[512,1024]{1,0:T(8,128)(2,1)}, bf16[512,1024]{1,0:T(8,128)(2,1)S(1)}, u32[]{:S(2)}, u32[]{:S(2)}) collective-permute-start(bf16[512,1024]{1,0:T(8,128)(2,1)} %get-tuple-element.33), channel_id=1, source_target_pairs={{0,8},{1,9},{2,10},{3,11},{4,12},{5,13},{6,14},{7,15},{8,0},{9,1},... | collective-permute-start | bytes 3145736 | tf_op jit(solution)/shard_map/ppermute | solution.py:23
  34.6 19.1 %collective-permute-start.4 = (bf16[256,1024]{1,0:T(8,128)(2,1)}, bf16[256,1024]{1,0:T(8,128)(2,1)S(1)}, u32[]{:S(2)}, u32[]{:S(2)}) collective-permute-start(bf16[256,1024]{1,0:T(8,128)(2,1)} %copy-done.6), channel_id=1, source_target_pairs={{0,6},{1,7},{2,0},{3,1},{4,2},{5,3},{6,4},{7,5},{8,14},{9,15},{10,... | collective-permute-start | bytes 1572872 | tf_op jit(solution)/shard_map/ppermute | solution.py:23
  53.7 16.3 %collective-permute-start.11 = (bf16[256,1024]{1,0:T(8,128)(2,1)}, bf16[256,1024]{1,0:T(8,128)(2,1)S(1)}, u32[]{:S(2)}, u32[]{:S(2)}) collective-permute-start(bf16[256,1024]{1,0:T(8,128)(2,1)} %get-tuple-element.34), channel_id=1, source_target_pairs={{0,2},{1,3},{2,4},{3,5},{4,6},{5,7},{6,0},{7,1},{8,10},{9,11},{10,... | collective-permute-start | bytes 1572872 | tf_op jit(solution)/shard_map/ppermute | solution.py:23
  53.7 23.5 %collective-permute-start.3 = (bf16[256,1024]{1,0:T(8,128)(2,1)S(1)}, bf16[256,1024]{1,0:T(8,128)(2,1)S(1)}, u32[]{:S(2)}, u32[]{:S(2)}) collective-permute-start(bf16[256,1024]{1,0:T(8,128)(2,1)S(1)} %copy-done.7), channel_id=1, source_target_pairs={{0,2},{1,3},{2,4},{3,5},{4,6},{5,7},{6,0},{7,1},{8,10},{9,11},{10,... | collective-permute-start | bytes 1572872 | tf_op jit(solution)/shard_map/ppermute | solution.py:23
  53.8 23.4 %collective-permute-start.5 = (bf16[256,1024]{1,0:T(8,128)(2,1)S(1)}, bf16[256,1024]{1,0:T(8,128)(2,1)}, u32[]{:S(2)}, u32[]{:S(2)}) collective-permute-start(bf16[256,1024]{1,0:T(8,128)(2,1)S(1)} %collective-permute-done.4.rest_2_), channel_id=1, source_target_pairs={{0,6},{1,7},{2,0},{3,1},{4,2},{5,3},{6,4},{7,5},{8,14},{9,15},{10,... | collective-permute-start | bytes 1572872 | tf_op jit(solution)/shard_map/ppermute | solution.py:23
  57.1 17.8 %all-to-all-start.1 = ((bf16[4,64,256]{2,1,0:T(8,128)(2,1)}), bf16[4,64,256]{2,1,0:T(8,128)(2,1)S(1)}, u32[]{:S(2)}, u32[]{:S(2)}) async-start(bf16[4,64,256]{2,1,0:T(8,128)(2,1)} %get-tuple-element.32), calls=%async_computation.1 | async-start | bytes 262144 | tf_op jit(solution)/shard_map/all_to_all | solution.py:439
  88.9 22.6 %collective-permute-start.12 = (bf16[512,3072]{1,0:T(8,128)(2,1)}, bf16[512,3072]{1,0:T(8,128)(2,1)S(1)}, u32[]{:S(2)}, u32[]{:S(2)}) collective-permute-start(bf16[512,3072]{1,0:T(8,128)(2,1)} %get-tuple-element.38), channel_id=1, source_target_pairs={{0,1},{1,0},{2,3},{3,2},{4,5},{5,4},{6,7},{7,6},{8,9},{9,8},{10,11... | collective-permute-start | bytes 9437192 | tf_op jit(solution)/shard_map/ppermute | solution.py:23
  89.0 33.5 %collective-permute-start.13 = (bf16[256,1024]{1,0:T(8,128)(2,1)}, bf16[256,1024]{1,0:T(8,128)(2,1)}, u32[]{:S(2)}, u32[]{:S(2)}) collective-permute-start(bf16[256,1024]{1,0:T(8,128)(2,1)} %get-tuple-element.42), channel_id=1, source_target_pairs={{0,8},{1,9},{2,10},{3,11},{4,12},{5,13},{6,14},{7,15},{8,0},{9,1},... | collective-permute-start | bytes 1572872 | tf_op jit(solution)/shard_map/ppermute | solution.py:23
  90.1 32.5 %collective-permute-start.15 = (bf16[256,1024]{1,0:T(8,128)(2,1)}, bf16[256,1024]{1,0:T(8,128)(2,1)}, u32[]{:S(2)}, u32[]{:S(2)}) collective-permute-start(bf16[256,1024]{1,0:T(8,128)(2,1)} %get-tuple-element.43), channel_id=1, source_target_pairs={{0,6},{1,7},{2,0},{3,1},{4,2},{5,3},{6,4},{7,5},{8,14},{9,15},{10,... | collective-permute-start | bytes 1572872 | tf_op jit(solution)/shard_map/ppermute | solution.py:23
  92.8 29.7 %collective-permute-start.14 = (bf16[256,1024]{1,0:T(8,128)(2,1)S(1)}, bf16[256,1024]{1,0:T(8,128)(2,1)}, u32[]{:S(2)}, u32[]{:S(2)}) collective-permute-start(bf16[256,1024]{1,0:T(8,128)(2,1)S(1)} %copy-done.10), channel_id=1, source_target_pairs={{0,2},{1,3},{2,4},{3,5},{4,6},{5,7},{6,0},{7,1},{8,10},{9,11},{10,... | collective-permute-start | bytes 1572872 | tf_op jit(solution)/shard_map/ppermute | solution.py:23
  92.9 14.2 %collective-permute-start.18 = (bf16[64,256]{1,0:T(8,128)(2,1)S(1)}, bf16[64,256]{1,0:T(8,128)(2,1)S(1)}, u32[]{:S(2)}, u32[]{:S(2)}) collective-permute-start(bf16[64,256]{1,0:T(8,128)(2,1)S(1)} %copy-done.15), channel_id=1, source_target_pairs={{0,48},{16,0},{32,16},{48,32},{64,112},{80,64},{96,80},{112,96},{1... | collective-permute-start | bytes 98312 | tf_op jit(solution)/shard_map/ppermute | solution.py:307
  107.0 10.6 %collective-permute-start.17 = (bf16[64,256]{1,0:T(8,128)(2,1)S(1)}, bf16[64,256]{1,0:T(8,128)(2,1)S(1)}, u32[]{:S(2)}, u32[]{:S(2)}) collective-permute-start(bf16[64,256]{1,0:T(8,128)(2,1)S(1)} %copy-done.15), channel_id=1, source_target_pairs={{0,32},{16,48},{32,0},{48,16},{64,96},{80,112},{96,64},{112,80},{1... | collective-permute-start | bytes 98312 | tf_op jit(solution)/shard_map/ppermute | solution.py:307
  111.5 6.1 %collective-permute-start.16 = (bf16[64,256]{1,0:T(8,128)(2,1)S(1)}, bf16[64,256]{1,0:T(8,128)(2,1)S(1)}, u32[]{:S(2)}, u32[]{:S(2)}) collective-permute-start(bf16[64,256]{1,0:T(8,128)(2,1)S(1)} %copy-done.15), channel_id=1, source_target_pairs={{0,16},{16,32},{32,48},{48,0},{64,80},{80,96},{96,112},{112,64},{1... | collective-permute-start | bytes 98312 | tf_op jit(solution)/shard_map/ppermute | solution.py:307
  119.9 6.5 %collective-permute-start.21 = (bf16[256,256]{1,0:T(8,128)(2,1)}, bf16[256,256]{1,0:T(8,128)(2,1)S(1)}, u32[]{:S(2)}, u32[]{:S(2)}) collective-permute-start(bf16[256,256]{1,0:T(8,128)(2,1)} %join_h.1.refs_4_.rest_0_), channel_id=1, source_target_pairs={{0,192},{16,208},{32,224},{48,240},{64,0},{80,16},{96,32},{112,48}... | collective-permute-start | bytes 393224 | tf_op jit(solution)/shard_map/ppermute | solution.py:307
  121.1 7.8 %collective-permute-start.20 = (bf16[256,256]{1,0:T(8,128)(2,1)}, bf16[256,256]{1,0:T(8,128)(2,1)S(1)}, u32[]{:S(2)}, u32[]{:S(2)}) collective-permute-start(bf16[256,256]{1,0:T(8,128)(2,1)} %join_h.1.refs_4_.rest_0_), channel_id=1, source_target_pairs={{0,128},{16,144},{32,160},{48,176},{64,192},{80,208},{96,224},{112... | collective-permute-start | bytes 393224 | tf_op jit(solution)/shard_map/ppermute | solution.py:307
  122.5 7.6 %collective-permute-start.19 = (bf16[256,256]{1,0:T(8,128)(2,1)}, bf16[256,256]{1,0:T(8,128)(2,1)S(1)}, u32[]{:S(2)}, u32[]{:S(2)}) collective-permute-start(bf16[256,256]{1,0:T(8,128)(2,1)} %join_h.1.refs_4_.rest_0_), channel_id=1, source_target_pairs={{0,64},{16,80},{32,96},{48,112},{64,128},{80,144},{96,160},{112,17... | collective-permute-start | bytes 393224 | tf_op jit(solution)/shard_map/ppermute | solution.py:307
  (22 other events, 85.5 us)

commit v2 on v1

--- a/solution.py
+++ b/solution.py
@@ -300,13 +300,6 @@
 WHOLE = pl.BlockSpec(memory_space=pltpu.VMEM)
 
 
-def shift_replica(a, dx=0, dh=0):
-    pairs = [
-        (x * NH + h, ((x + dx) % NX) * NH + (h + dh) % NH) for x in range(NX) for h in range(NH)
-    ]
-    return lax.ppermute(a, "replica", pairs)
-
-
 def small_call(body, n_in, after, out_shape, scratch, name):
     return pl.pallas_call(
         body,
@@ -323,26 +316,25 @@
 H_GROUPS = [[x * NH + h for h in range(NH)] for x in range(NX)]
 
 
-def sum_along_x(here, parts, after):
-    _, rows, wide = parts.shape
-    thin = wide // NH
+def sum_along_h(here, parts, after):
+    _, wide, rows = parts.shape
 
     def body(here_ref, p_ref, *rest):
         out_ref = rest[len(after)]
         acc = p_ref[0].astype(F32)
-        for k in range(1, NX):
+        for k in range(1, NH):
             acc += p_ref[k].astype(F32)
-        out_ref[...] = acc.T.astype(BF16).reshape(NH, thin, rows)
-
-    out = [jax.ShapeDtypeStruct((NH, thin, rows), BF16)]
-    return small_call(body, 1, after, out, [], "sum_along_x")(here, parts, *after)[0]
+        out_ref[...] = acc.astype(BF16).reshape(out_ref.shape)
+
+    out = [jax.ShapeDtypeStruct((NX, wide // NX, rows), BF16)]
+    return small_call(body, 1, after, out, [], "sum_along_h")(here, parts, *after)[0]
 
 
 def outer_step(here, parts, params, moment, after):
     def body(here_ref, t_ref, p_ref, m_ref, *rest):
         np_ref, nm_ref, s_ref = rest[len(after) :]
         total = t_ref[0].astype(F32)
-        for k in range(1, NH):
+        for k in range(1, NX):
             total += t_ref[k].astype(F32)
         p = p_ref[...]
         pseudo = p - total / (NX * NH)
@@ -350,59 +342,35 @@
         new = p - 0.7 * (pseudo + 0.9 * nm)
         nm_ref[...] = nm
         np_ref[...] = new
-        s_ref[...] = new.astype(BF16)
-
-    out = [jax.ShapeDtypeStruct(params.shape, d) for d in (F32, F32, BF16)]
+        s_ref[...] = jnp.broadcast_to(new.astype(BF16)[None], s_ref.shape)
+
+    out = [jax.ShapeDtypeStruct(params.shape, F32)] * 2
+    out.append(jax.ShapeDtypeStruct((NH,) + params.shape, BF16))
     return small_call(body, 3, after, out, [], "outer_step")(here, parts, params, moment, *after)
 
 
 def join_h(here, parts, after):
-    thin, rows = parts[0].shape
-
-    def body(here_ref, *rest):
-        part_refs, out_ref, total = rest[:NH], rest[-2], rest[-1]
-        h = here_ref[1] % NH
-        for k in range(NH):
-            at = pl.multiple_of(((h + NH - k) % NH) * thin, thin)
-            total[pl.ds(at, thin), :] = part_refs[k][...].astype(F32)
-        out_ref[...] = total[...].T.astype(BF16)
-
-    return small_call(
-        body,
-        NH,
-        after,
-        [jax.ShapeDtypeStruct((rows, NH * thin), BF16)],
-        [pltpu.VMEM((NH * thin, rows), F32)],
-        "join_h",
-    )(here, *parts, *after)[0]
+    _, thin, rows = parts.shape
+
+    def body(here_ref, p_ref, *rest):
+        out_ref = rest[len(after)]
+        one = p_ref[...].astype(F32).reshape(NH * thin, rows).T.astype(BF16)
+        out_ref[...] = jnp.broadcast_to(one[None], out_ref.shape)
+
+    out = [jax.ShapeDtypeStruct((NX, rows, NH * thin), BF16)]
+    return small_call(body, 1, after, out, [], "join_h")(here, parts, *after)[0]
 
 
 def join_x(here, parts, after):
-    rows, wide = parts[0].shape
-
-    def body(here_ref, *rest):
-        part_refs, out_ref, sems = rest[:NX], rest[-2], rest[-1]
-        x = here_ref[1] // NH
-        copies = [
-            pltpu.make_async_copy(
-                part_refs[k], columns(out_ref, (x + NX - k) % NX, wide), sems.at[k]
-            )
-            for k in range(NX)
-        ]
-        for c in copies:
-            c.start()
-        for c in copies:
-            c.wait()
-
-    return pl.pallas_call(
-        body,
-        in_specs=[SMEM] + [WHOLE] * NX + [ANY] * len(after),
-        out_specs=ANY,
-        out_shape=jax.ShapeDtypeStruct((rows, NX * wide), BF16),
-        scratch_shapes=[pltpu.SemaphoreType.DMA((NX,))],
-        compiler_params=pltpu.CompilerParams(vmem_limit_bytes=VMEM_LIMIT),
-        name="join_x",
-    )(here, *parts, *after)
+    _, rows, wide = parts.shape
+
+    def body(here_ref, p_ref, *rest):
+        out_ref = rest[len(after)]
+        for k in range(NX):
+            out_ref[:, k * wide : (k + 1) * wide] = p_ref[k]
+
+    out = [jax.ShapeDtypeStruct((rows, NX * wide), BF16)]
+    return small_call(body, 1, after, out, [], "join_x")(here, parts, *after)[0]
 
 
 def on_device(tokens, kv_cotangent, inner_weights, outer_params, outer_momentum):
@@ -416,27 +384,36 @@
     tok_rx = shift_fsdp(tok, dc=1)
     cot_rx = shift_fsdp(cot, dc=1)
 
-    parts = w.reshape(w.shape[0], NX, w.shape[1] // NX).transpose(1, 0, 2)
-    parts = lax.all_to_all(parts, "replica", 0, 0, axis_index_groups=X_GROUPS, tiled=True)
-    sum_x = sum_along_x(here, parts, ())
+    thin = w.shape[1] // (NX * NH)
+    parts = w.T.reshape(NX, NH, thin, w.shape[0]).transpose(1, 0, 2, 3)
+    parts = parts.reshape(NH, NX * thin, w.shape[0])
+    parts = lax.all_to_all(parts, "replica", 0, 0, axis_index_groups=H_GROUPS, tiled=True)
 
     w_op = shift_fsdp(w_dn, dy=1)
     wz_up = shift_fsdp(w_z, dy=-1)
     wz_dn = shift_fsdp(w_z, dy=1)
     wz_op = shift_fsdp(wz_up, dy=-1)
 
-    g1, g2, g3 = far_gradients(here, tok, tok_rx, cot, cot_rx, (sum_x, w_dn, w_up, w_z))
+    g1, g2, g3 = far_gradients(here, tok, tok_rx, cot, cot_rx, (w_dn, w_up))
     r1 = shift_fsdp(g1, dz=1)
     r2 = shift_fsdp(g2, dz=1)
     r3 = shift_fsdp(g3, dz=1)
 
+    sum_h = sum_along_h(here, parts, (g1,))
+    total = lax.all_to_all(sum_h, "replica", 0, 0, axis_index_groups=X_GROUPS, tiled=True)
+
     steps = (0, NY - 1, 1, 2)
     kv_own, grads, to_core, kv_send, own = project(
-        here, tok, tok_rx, cot, cot_rx, [w, w_dn, w_up, w_op], steps, after=(g1,)
-    )
-
-    to_up, sum_x = add_blocks(own, [(3, [(r1, 0)])], BF16, along=(sum_x,))
-    total = lax.all_to_all(sum_x, "replica", 0, 0, axis_index_groups=H_GROUPS, tiled=True)
+        here, tok, tok_rx, cot, cot_rx, [w, w_dn, w_up, w_op], steps, after=(sum_h,)
+    )
+
+    new_params, new_moment, synced = outer_step(
+        here, total, outer_params.T, outer_momentum.T, (own,)
+    )
+    ready = synced
+    synced = lax.all_to_all(synced, "replica", 0, 0, axis_index_groups=H_GROUPS, tiled=True)
+
+    (to_up,) = add_blocks(own, [(3, [(r1, 0)])], BF16, (ready, wz_dn, wz_up))
     two_down = shift_fsdp(to_up, dy=1)
 
     to_up, to_dn = add_blocks(
@@ -445,10 +422,9 @@
     from_dn = shift_fsdp(to_up, dy=1)
     from_up = shift_fsdp(to_dn, dy=-1)
 
-    new_params, new_moment, synced = outer_step(
-        here, total, outer_params.T, outer_momentum.T, (to_up,)
-    )
-    synced = [synced] + [shift_replica(synced, dh=k) for k in range(1, NH)]
+    ready = join_h(here, synced, (to_up,))
+    synced = lax.all_to_all(ready, "replica", 0, 0, axis_index_groups=X_GROUPS, tiled=True)
+
     kv_own, grads, to_core = project(
         here,
         tok,
@@ -458,16 +434,14 @@
         [w_z, wz_dn, wz_up, wz_op],
         steps,
         (kv_own, kv_send, grads, to_core),
-        after=(synced[0],),
+        after=(ready,),
     )
     other_rx = shift_fsdp(to_core, dc=1)
     keys_values, token_grads = merge(here, kv_own, other_rx, grads, steps, (kv_own,))
-    synced = join_h(here, synced, (keys_values,))
-    synced = [synced] + [shift_replica(synced, dx=k) for k in range(1, NX)]
+    synced = join_x(here, synced, (keys_values,))
     (weight_grads,) = add_blocks(
-        own, [(0, [(r3, 0), (from_dn, 0), (from_up, 0)])], F32, (synced[0],)
-    )
-    synced = join_x(here, synced, (weight_grads,))
+        own, [(0, [(r3, 0), (from_dn, 0), (from_up, 0)])], F32, (synced,)
+    )
 
     return (
         keys_values[None],

time: 134 us -> 115 us (0.86)
  waiting for transfers between devices: 28.6 us -> 8.44 us
  starting transfers between devices: 40.4 us -> 44.4 us
  local copies, waits for them, and re-layouts: 12.2 us -> 9.84 us
    all_to_all x2 -> x4, starting transfers between devices: 10.8 us -> 25.9 us  [the longest x1 10 us: on_device(): lax.all_to_all(synced, 'replica', 0, 0, axis_index_groups=H_GROUPS, tiled...]
    ppermute x6 -> x0, waiting for transfers between devices: 14.5 us -> none  [shift_replica(): return lax.ppermute(a, 'replica', pairs)]
    ppermute x6 -> x0, starting transfers between devices: 11.6 us -> none  [shift_replica(): return lax.ppermute(a, 'replica', pairs)]
    ppermute x16, waiting for transfers between devices: 5.63 us -> 1.66 us  [shift_fsdp(): return lax.ppermute(a, 'fsdp', pairs)]
    unnamed x45 -> x24, local copies, waits for them, and re-layouts: 11.2 us -> 7.73 us
    transpose x0 -> x2, local copies, waits for them, and re-layouts: none -> 2.11 us  [on_device(): parts = w.T.reshape(NX, NH, thin, w.shape[0]).transpose(1, 0, 2, 3)]
    all_to_all x2 -> x4, waiting for transfers between devices: 8.51 us -> 6.78 us  [the longest x1 3.5 us: on_device(): lax.all_to_all(synced, 'replica', 0, 0, axis_index_groups=H_GROUPS, tiled...]
  transfers between devices with their start and end apart: 24 -> 20, of which waited for: 6 -> 5; matrix products, arithmetic and copies ran while one was open for 2% -> 2% of each run, Pallas kernels for 28% -> 32%
where the time goes in v2:
time: 115 us; the launch traced here: 114 us
  Pallas kernels  50 us (43%)
  starting transfers between devices  44.4 us (39%)
  local copies, waits for them, and re-layouts  9.84 us (9%)
  waiting for transfers between devices  8.44 us (7%)
    pallas_call x2, Pallas kernels, project(): pl.pallas_call(body, in_specs=[SMEM] + [ANY] * (len(args) - 1), out_specs...  22.9 us
    ppermute x16, starting transfers between devices, shift_fsdp(): return lax.ppermute(a, 'fsdp', pairs)  18.5 us
    all_to_all x1, starting transfers between devices, on_device(): lax.all_to_all(synced, 'replica', 0, 0, axis_index_groups=H_GROUPS, tiled...  10 us
    pallas_call x3, Pallas kernels, add_blocks(): pl.pallas_call(body, grid=(1,), in_specs=[spec(k) for _, k, _ in flat] +...  8.23 us
    unnamed x24, local copies, waits for them, and re-layouts  7.73 us
    pallas_call x1, Pallas kernels, far_gradients(): pl.pallas_call(body, grid_spec=pltpu.PrefetchScalarGridSpec(num_scalar_pr...  7.25 us
    all_to_all x1, starting transfers between devices, on_device(): lax.all_to_all(parts, 'replica', 0, 0, axis_index_groups=H_GROUPS, tiled=...  6.72 us
    all_to_all x1, starting transfers between devices, on_device(): lax.all_to_all(ready, 'replica', 0, 0, axis_index_groups=X_GROUPS, tiled=...  4.79 us
  transfers between devices with their start and end apart: 20, of which 5 were waited for; matrix products, arithmetic and copies ran while one was open for 2% of the time, Pallas kernels for 32%

profile of v2, /device:TPU:32, one launch (start us, length us, event | category | flops | bytes accessed | tf_op | source)
XLA Modules:
  0.0 114.1 jit_solution(2076757817271467136)
XLA Ops:
  1.2 1.6 %collective-permute-start.6 = (bf16[256,1024]{1,0:T(8,128)(2,1)}, bf16[256,1024]{1,0:T(8,128)(2,1)S(1)}, u32[]{:S(2)}, u32[]{:S(2)}) collective-permute-start(bf16[256,1024]{1,0:T(8,128)(2,1)} %bitcast.27), channel_id=1, source_target_pairs={{0,2},{1,3},{2,4},{3,5},{4,6},{5,7},{6,0},{7,1},{8,10},{9,11},{10,... | collective-permute-start | bytes 1572872 | tf_op jit(solution)/shard_map/ppermute | solution.py:23
  3.1 3.2 %collective-permute-start.7 = (bf16[256,1024]{1,0:T(8,128)(2,1)}, bf16[256,1024]{1,0:T(8,128)(2,1)S(1)}, u32[]{:S(2)}, u32[]{:S(2)}) collective-permute-start(bf16[256,1024]{1,0:T(8,128)(2,1)} %bitcast.29), channel_id=1, source_target_pairs={{0,6},{1,7},{2,0},{3,1},{4,2},{5,3},{6,4},{7,5},{8,14},{9,15},{10,... | collective-permute-start | bytes 1572872 | tf_op jit(solution)/shard_map/ppermute | solution.py:23
  8.4 6.7 %all-to-all-start = ((bf16[4,256,256]{2,1,0:T(8,128)(2,1)}), bf16[4,256,256]{2,1,0:T(8,128)(2,1)}, u32[]{:S(2)}, u32[]{:S(2)}) async-start(bf16[4,256,256]{2,1,0:T(8,128)(2,1)} %bitcast.8), calls=%async_computation | async-start | bytes 1048576 | tf_op jit(solution)/shard_map/all_to_all | solution.py:390
  17.6 2.9 %collective-permute-start.4 = (bf16[256,1024]{1,0:T(8,128)(2,1)}, bf16[256,1024]{1,0:T(8,128)(2,1)S(1)}, u32[]{:S(2)}, u32[]{:S(2)}) collective-permute-start(bf16[256,1024]{1,0:T(8,128)(2,1)} %collective-permute-done.2.rest_0_), channel_id=1, source_target_pairs={{0,6},{1,7},{2,0},{3,1},{4,2},{5,3},{6,4},{7,5},{8,14},{9,15},{10,... | collective-permute-start | bytes 1572872 | tf_op jit(solution)/shard_map/ppermute | solution.py:23
  21.7 7.3 %far_gradients.1 = (bf16[256,1024]{1,0:T(8,128)(2,1)}, bf16[512,1024]{1,0:T(8,128)(2,1)}, bf16[256,1024]{1,0:T(8,128)(2,1)}) custom-call(s32[2]{0:T(128)} %pad_add_fusion.here_ref, bf16[512,4096]{1,0:T(8,128)(2,1)} %bitcast.19, bf16[512,4096]{1,0:T(8,128)(2,1)} %collective-permute-done.tr_ref.tx_ref, bf16[512,1024]{1,0:T(8,128)(2,1)} %bitcast.24, ...), custom_call_target="tpu_custom_call" | custom-call | tf_op jit(solution)/shard_map/far_gradients/pallas_call | solution.py:75
  28.9 1.8 %collective-permute-start.10 = (bf16[256,1024]{1,0:T(8,128)(2,1)}, bf16[256,1024]{1,0:T(8,128)(2,1)S(1)}, u32[]{:S(2)}, u32[]{:S(2)}) collective-permute-start(bf16[256,1024]{1,0:T(8,128)(2,1)} %get-tuple-element.24.rest_0_), channel_id=1, source_target_pairs={{0,8},{1,9},{2,10},{3,11},{4,12},{5,13},{6,14},{7,15},{8,0},{9,1},... | collective-permute-start | bytes 1572872 | tf_op jit(solution)/shard_map/ppermute | solution.py:23
  31.0 1.8 %sum_along_h.1.rest_4_ = bf16[4,64,256]{2,1,0:T(8,128)(2,1)} custom-call(s32[2]{0:T(128)} %pad_add_fusion.here_ref, bf16[4,256,256]{2,1,0:T(8,128)(2,1)} %all-to-all-done.p_ref, bf16[256,1024]{1,0:T(8,128)(2,1)} %get-tuple-element.24.rest_0_), custom_call_target="tpu_custom_call" | custom-call | tf_op jit(solution)/shard_map/sum_along_h/pallas_call | solution.py:330
  32.8 4.3 %all-to-all-start.1 = ((bf16[4,64,256]{2,1,0:T(8,128)(2,1)}), bf16[4,64,256]{2,1,0:T(8,128)(2,1)S(1)}, u32[]{:S(2)}, u32[]{:S(2)}) async-start(bf16[4,64,256]{2,1,0:T(8,128)(2,1)} %sum_along_h.1.rest_4_), calls=%async_computation.1 | async-start | bytes 262144 | tf_op jit(solution)/shard_map/all_to_all | solution.py:403
  37.1 12.2 %project.2 = (f32[512,1024]{1,0:T(8,128)}, bf16[512,4096]{1,0:T(8,128)(2,1)}, bf16[512,3072]{1,0:T(8,128)(2,1)}, f32[512,1024]{1,0:T(8,128)}, f32[1024,1024]{1,0:T(8,128)}) custom-call(s32[2]{0:T(128)} %pad_add_fusion.here_ref, bf16[512,4096]{1,0:T(8,128)(2,1)} %bitcast.20, bf16[512,4096]{1,0:T(8,128)(2,1)} %collective-permute-done.tr_ref.tx_ref, ...), custom_call_target="tpu_custom_call" | custom-call | tf_op jit(solution)/shard_map/project/pallas_call | solution.py:237
  50.0 1.7 %outer_step.1 = (f32[64,256]{1,0:T(8,128)}, f32[64,256]{1,0:T(8,128)}, bf16[4,64,256]{2,1,0:T(8,128)(2,1)}) custom-call(s32[2]{0:T(128)} %pad_add_fusion.here_ref, bf16[4,64,256]{2,1,0:T(8,128)(2,1)} %copy-done.9, f32[64,256]{1,0:T(8,128)} %bitcast.35, f32[64,256]{1,0:T(8,128)} %bitcast.36, f32[1024,1024]{1,0:T(8,128)} %get-tuple-element.29.rest_0_.refs_0_.refs_1_), custom_call_target="tpu_custom_call" | custom-call | tf_op jit(solution)/shard_map/outer_step/pallas_call | solution.py:349
  52.8 2.2 %add_blocks.3 = bf16[256,1024]{1,0:T(8,128)(2,1)} custom-call(f32[1024,1024]{1,0:T(8,128)} %get-tuple-element.29.rest_0_.refs_0_.refs_1_, bf16[256,1024]{1,0:T(8,128)(2,1)} %copy-done.7, bf16[4,64,256]{2,1,0:T(8,128)(2,1)} %get-tuple-element.30.refs_2_, bf16[256,1024]{1,0:T(8,128)(2,1)} %copy-done.4, bf16[256,1024]{1,0:T(8,128)(2,1)} %copy-done.3), custom_call_target="tpu_custom_call" | custom-call | tf_op jit(solution)/shard_map/add_blocks/pallas_call | solution.py:117
  56.3 2.0 %collective-permute-start.5 = (bf16[256,1024]{1,0:T(8,128)(2,1)}, bf16[256,1024]{1,0:T(8,128)(2,1)S(1)}, u32[]{:S(2)}, u32[]{:S(2)}) collective-permute-start(bf16[256,1024]{1,0:T(8,128)(2,1)} %copy-done.3), channel_id=1, source_target_pairs={{0,6},{1,7},{2,0},{3,1},{4,2},{5,3},{6,4},{7,5},{8,14},{9,15},{10,... | collective-permute-start | bytes 1572872 | tf_op jit(solution)/shard_map/ppermute | solution.py:23
  58.2 10.0 %all-to-all-start.2 = ((bf16[4,64,256]{2,1,0:T(8,128)(2,1)}), bf16[4,64,256]{2,1,0:T(8,128)(2,1)S(1)}, u32[]{:S(2)}, u32[]{:S(2)}) async-start(bf16[4,64,256]{2,1,0:T(8,128)(2,1)} %get-tuple-element.30.refs_2_), calls=%async_computation.2 | async-start | bytes 262144 | tf_op jit(solution)/shard_map/all_to_all | solution.py:414
  70.2 3.1 %add_blocks.4 = (bf16[256,1024]{1,0:T(8,128)(2,1)}, bf16[256,1024]{1,0:T(8,128)(2,1)}) custom-call(f32[1024,1024]{1,0:T(8,128)} %get-tuple-element.29.rest_0_.refs_0_.refs_1_, f32[1024,1024]{1,0:T(8,128)} %get-tuple-element.29.rest_0_.refs_0_.refs_1_, bf16[512,1024]{1,0:T(8,128)(2,1)} %copy-done.1, bf16[256,1024]{1,0:T(8,128)(2,1)} %copy-done.11, ...), custom_call_target="tpu_custom_call" | custom-call | tf_op jit(solution)/shard_map/add_blocks/pallas_call | solution.py:117
  73.3 3.5 %all-to-all-done.2.p_ref = bf16[4,64,256]{2,1,0:T(8,128)(2,1)S(1)} async-done(((bf16[4,64,256]{2,1,0:T(8,128)(2,1)}), bf16[4,64,256]{2,1,0:T(8,128)(2,1)S(1)}, u32[]{:S(2)}, u32[]{:S(2)}) %all-to-all-start.2) | async-done | bytes 131104 | tf_op jit(solution)/shard_map/all_to_all | solution.py:414
  77.5 1.8 %join_h.1.rest_8_ = bf16[4,256,256]{2,1,0:T(8,128)(2,1)} custom-call(s32[2]{0:T(128)} %pad_add_fusion.here_ref, bf16[4,64,256]{2,1,0:T(8,128)(2,1)} %copy-done.10, bf16[256,1024]{1,0:T(8,128)(2,1)} %get-tuple-element.32.rest_0_), custom_call_target="tpu_custom_call" | custom-call | tf_op jit(solution)/shard_map/join_h/pallas_call | solution.py:361
  80.1 10.7 %project.3 = (f32[512,1024]{1,0:T(8,128)}, bf16[512,4096]{1,0:T(8,128)(2,1)}, bf16[512,3072]{1,0:T(8,128)(2,1)}) custom-call(s32[2]{0:T(128)} %pad_add_fusion.here_ref, bf16[512,4096]{1,0:T(8,128)(2,1)} %bitcast.21, bf16[512,4096]{1,0:T(8,128)(2,1)} %collective-permute-done.tr_ref.tx_ref, ...), custom_call_target="tpu_custom_call", output_to_operand_aliasing={{1}: (11, {}), {2}: (12, {})} | custom-call | tf_op jit(solution)/shard_map/project/pallas_call | solution.py:237
  91.0 2.2 %collective-permute-start.13 = (bf16[256,1024]{1,0:T(8,128)(2,1)}, bf16[256,1024]{1,0:T(8,128)(2,1)}, u32[]{:S(2)}, u32[]{:S(2)}) collective-permute-start(bf16[256,1024]{1,0:T(8,128)(2,1)} %get-tuple-element.38), channel_id=1, source_target_pairs={{0,8},{1,9},{2,10},{3,11},{4,12},{5,13},{6,14},{7,15},{8,0},{9,1},... | collective-permute-start | bytes 1572872 | tf_op jit(solution)/shard_map/ppermute | solution.py:23
  95.2 4.8 %all-to-all-start.3 = ((bf16[4,256,256]{2,1,0:T(8,128)(2,1)}), bf16[4,256,256]{2,1,0:T(8,128)(2,1)}, u32[]{:S(2)}, u32[]{:S(2)}) async-start(bf16[4,256,256]{2,1,0:T(8,128)(2,1)} %join_h.1.rest_8_), calls=%async_computation.3 | async-start | bytes 1048576 | tf_op jit(solution)/shard_map/all_to_all | solution.py:426
  100.0 1.6 %copy-done.2 = bf16[512,3072]{1,0:T(8,128)(2,1)} copy-done((bf16[512,3072]{1,0:T(8,128)(2,1)}, bf16[512,3072]{1,0:T(8,128)(2,1)S(1)}, u32[]{:S(2)}) %copy-start.2) | copy-done | bytes 3145752
  101.6 4.5 %merge.1 = (bf16[512,1024]{1,0:T(8,128)(2,1)}, bf16[512,4096]{1,0:T(8,128)(2,1)}) custom-call(s32[2]{0:T(128)} %pad_add_fusion.here_ref, f32[512,1024]{1,0:T(8,128)} %get-tuple-element.33.own_ref.rest_0_, bf16[512,3072]{1,0:T(8,128)(2,1)} %copy-done.2, bf16[512,4096]{1,0:T(8,128)(2,1)} %get-tuple-element.35._, ...), custom_call_target="tpu_custom_call", output_to_operand_aliasing={{1}: (3, {})} | custom-call | tf_op jit(solution)/shard_map/merge/pallas_call | solution.py:280
  106.1 3.2 %all-to-all-done.3.p_ref = bf16[4,256,256]{2,1,0:T(8,128)(2,1)} async-done(((bf16[4,256,256]{2,1,0:T(8,128)(2,1)}), bf16[4,256,256]{2,1,0:T(8,128)(2,1)}, u32[]{:S(2)}, u32[]{:S(2)}) %all-to-all-start.3) | async-done | bytes 524320 | tf_op jit(solution)/shard_map/all_to_all | solution.py:426
  109.3 1.9 %join_x.1.refs_4_ = bf16[256,1024]{1,0:T(8,128)(2,1)} custom-call(s32[2]{0:T(128)} %pad_add_fusion.here_ref, bf16[4,256,256]{2,1,0:T(8,128)(2,1)} %all-to-all-done.3.p_ref, bf16[512,1024]{1,0:T(8,128)(2,1)} %get-tuple-element.36.rest_0_), custom_call_target="tpu_custom_call" | custom-call | tf_op jit(solution)/shard_map/join_x/pallas_call | solution.py:373
  111.3 2.9 %add_blocks.5 = f32[256,1024]{1,0:T(8,128)} custom-call(f32[1024,1024]{1,0:T(8,128)} %get-tuple-element.29.rest_0_.refs_0_.refs_1_, bf16[256,1024]{1,0:T(8,128)(2,1)} %collective-permute-done.13.refs_1_, bf16[256,1024]{1,0:T(8,128)(2,1)} %collective-permute-done.14.refs_2_, bf16[256,1024]{1,0:T(8,128)(2,1)} %collective-permute-done.15.refs_3_, ...), custom_call_target="tpu_custom_call" | custom-call | tf_op jit(solution)/shard_map/add_blocks/pallas_call | solution.py:117
  (54 shorter events, 15.4 us)
Async XLA Ops:
  0.6 19.9 %collective-permute-start = (bf16[512,4096]{1,0:T(8,128)(2,1)}, bf16[512,4096]{1,0:T(8,128)(2,1)}, u32[]{:S(2)}, u32[]{:S(2)}) collective-permute-start(bf16[512,4096]{1,0:T(8,128)(2,1)} %bitcast.18), channel_id=1, source_target_pairs={{0,1},{1,0},{2,3},{3,2},{4,5},{5,4},{6,7},{7,6},{8,9},{9,8},{10,11... | collective-permute-start | bytes 12582920 | tf_op jit(solution)/shard_map/ppermute | solution.py:23
  0.7 19.8 %collective-permute-start.1 = (bf16[512,1024]{1,0:T(8,128)(2,1)}, bf16[512,1024]{1,0:T(8,128)(2,1)S(1)}, u32[]{:S(2)}, u32[]{:S(2)}) collective-permute-start(bf16[512,1024]{1,0:T(8,128)(2,1)} %bitcast.23), channel_id=1, source_target_pairs={{0,1},{1,0},{2,3},{3,2},{4,5},{5,4},{6,7},{7,6},{8,9},{9,8},{10,11... | collective-permute-start | bytes 3145736 | tf_op jit(solution)/shard_map/ppermute | solution.py:23
  1.2 15.4 %collective-permute-start.6 = (bf16[256,1024]{1,0:T(8,128)(2,1)}, bf16[256,1024]{1,0:T(8,128)(2,1)S(1)}, u32[]{:S(2)}, u32[]{:S(2)}) collective-permute-start(bf16[256,1024]{1,0:T(8,128)(2,1)} %bitcast.27), channel_id=1, source_target_pairs={{0,2},{1,3},{2,4},{3,5},{4,6},{5,7},{6,0},{7,1},{8,10},{9,11},{10,... | collective-permute-start | bytes 1572872 | tf_op jit(solution)/shard_map/ppermute | solution.py:23
  2.8 14.8 %collective-permute-start.2 = (bf16[256,1024]{1,0:T(8,128)(2,1)}, bf16[256,1024]{1,0:T(8,128)(2,1)}, u32[]{:S(2)}, u32[]{:S(2)}) collective-permute-start(bf16[256,1024]{1,0:T(8,128)(2,1)} %bitcast.28), channel_id=1, source_target_pairs={{0,8},{1,9},{2,10},{3,11},{4,12},{5,13},{6,14},{7,15},{8,0},{9,1},... | collective-permute-start | bytes 1572872 | tf_op jit(solution)/shard_map/ppermute | solution.py:23
  3.1 17.5 %collective-permute-start.7 = (bf16[256,1024]{1,0:T(8,128)(2,1)}, bf16[256,1024]{1,0:T(8,128)(2,1)S(1)}, u32[]{:S(2)}, u32[]{:S(2)}) collective-permute-start(bf16[256,1024]{1,0:T(8,128)(2,1)} %bitcast.29), channel_id=1, source_target_pairs={{0,6},{1,7},{2,0},{3,1},{4,2},{5,3},{6,4},{7,5},{8,14},{9,15},{10,... | collective-permute-start | bytes 1572872 | tf_op jit(solution)/shard_map/ppermute | solution.py:23
  8.4 22.6 %all-to-all-start = ((bf16[4,256,256]{2,1,0:T(8,128)(2,1)}), bf16[4,256,256]{2,1,0:T(8,128)(2,1)}, u32[]{:S(2)}, u32[]{:S(2)}) async-start(bf16[4,256,256]{2,1,0:T(8,128)(2,1)} %bitcast.8), calls=%async_computation | async-start | bytes 1048576 | tf_op jit(solution)/shard_map/all_to_all | solution.py:390
  16.6 3.9 %copy-start.5 = (bf16[256,1024]{1,0:T(8,128)(2,1)}, bf16[256,1024]{1,0:T(8,128)(2,1)S(1)}, u32[]{:S(2)}) copy-start(bf16[256,1024]{1,0:T(8,128)(2,1)S(1)} %collective-permute-done.6.rest_0_.rest_1_) | copy-start | bytes 1572868
  16.6 20.5 %collective-permute-start.8 = (bf16[256,1024]{1,0:T(8,128)(2,1)S(1)}, bf16[256,1024]{1,0:T(8,128)(2,1)}, u32[]{:S(2)}, u32[]{:S(2)}) collective-permute-start(bf16[256,1024]{1,0:T(8,128)(2,1)S(1)} %collective-permute-done.6.rest_0_.rest_1_), channel_id=1, source_target_pairs={{0,2},{1,3},{2,4},{3,5},{4,6},{5,7},{6,0},{7,1},{8,10},{9,11},{10,... | collective-permute-start | bytes 1572872 | tf_op jit(solution)/shard_map/ppermute | solution.py:23
  17.6 34.0 %collective-permute-start.4 = (bf16[256,1024]{1,0:T(8,128)(2,1)}, bf16[256,1024]{1,0:T(8,128)(2,1)S(1)}, u32[]{:S(2)}, u32[]{:S(2)}) collective-permute-start(bf16[256,1024]{1,0:T(8,128)(2,1)} %collective-permute-done.2.rest_0_), channel_id=1, source_target_pairs={{0,6},{1,7},{2,0},{3,1},{4,2},{5,3},{6,4},{7,5},{8,14},{9,15},{10,... | collective-permute-start | bytes 1572872 | tf_op jit(solution)/shard_map/ppermute | solution.py:23
  20.5 31.1 %collective-permute-start.3 = (bf16[256,1024]{1,0:T(8,128)(2,1)}, bf16[256,1024]{1,0:T(8,128)(2,1)S(1)}, u32[]{:S(2)}, u32[]{:S(2)}) collective-permute-start(bf16[256,1024]{1,0:T(8,128)(2,1)} %collective-permute-done.2.rest_0_), channel_id=1, source_target_pairs={{0,2},{1,3},{2,4},{3,5},{4,6},{5,7},{6,0},{7,1},{8,10},{9,11},{10,... | collective-permute-start | bytes 1572872 | tf_op jit(solution)/shard_map/ppermute | solution.py:23
  20.6 1.1 copy-start
  28.9 22.7 %collective-permute-start.10 = (bf16[256,1024]{1,0:T(8,128)(2,1)}, bf16[256,1024]{1,0:T(8,128)(2,1)S(1)}, u32[]{:S(2)}, u32[]{:S(2)}) collective-permute-start(bf16[256,1024]{1,0:T(8,128)(2,1)} %get-tuple-element.24.rest_0_), channel_id=1, source_target_pairs={{0,8},{1,9},{2,10},{3,11},{4,12},{5,13},{6,14},{7,15},{8,0},{9,1},... | collective-permute-start | bytes 1572872 | tf_op jit(solution)/shard_map/ppermute | solution.py:23
  30.7 37.7 %collective-permute-start.9 = (bf16[512,1024]{1,0:T(8,128)(2,1)}, bf16[512,1024]{1,0:T(8,128)(2,1)S(1)}, u32[]{:S(2)}, u32[]{:S(2)}) collective-permute-start(bf16[512,1024]{1,0:T(8,128)(2,1)} %get-tuple-element.31), channel_id=1, source_target_pairs={{0,8},{1,9},{2,10},{3,11},{4,12},{5,13},{6,14},{7,15},{8,0},{9,1},... | collective-permute-start | bytes 3145736 | tf_op jit(solution)/shard_map/ppermute | solution.py:23
  32.8 16.5 %all-to-all-start.1 = ((bf16[4,64,256]{2,1,0:T(8,128)(2,1)}), bf16[4,64,256]{2,1,0:T(8,128)(2,1)S(1)}, u32[]{:S(2)}, u32[]{:S(2)}) async-start(bf16[4,64,256]{2,1,0:T(8,128)(2,1)} %sum_along_h.1.rest_4_), calls=%async_computation.1 | async-start | bytes 262144 | tf_op jit(solution)/shard_map/all_to_all | solution.py:403
  51.7 1.1 copy-start.7
  55.0 13.4 %collective-permute-start.11 = (bf16[256,1024]{1,0:T(8,128)(2,1)}, bf16[256,1024]{1,0:T(8,128)(2,1)S(1)}, u32[]{:S(2)}, u32[]{:S(2)}) collective-permute-start(bf16[256,1024]{1,0:T(8,128)(2,1)} %add_blocks.3), channel_id=1, source_target_pairs={{0,2},{1,3},{2,4},{3,5},{4,6},{5,7},{6,0},{7,1},{8,10},{9,11},{10,... | collective-permute-start | bytes 1572872 | tf_op jit(solution)/shard_map/ppermute | solution.py:23
  56.3 23.0 %collective-permute-start.5 = (bf16[256,1024]{1,0:T(8,128)(2,1)}, bf16[256,1024]{1,0:T(8,128)(2,1)S(1)}, u32[]{:S(2)}, u32[]{:S(2)}) collective-permute-start(bf16[256,1024]{1,0:T(8,128)(2,1)} %copy-done.3), channel_id=1, source_target_pairs={{0,6},{1,7},{2,0},{3,1},{4,2},{5,3},{6,4},{7,5},{8,14},{9,15},{10,... | collective-permute-start | bytes 1572872 | tf_op jit(solution)/shard_map/ppermute | solution.py:23
  58.2 18.6 %all-to-all-start.2 = ((bf16[4,64,256]{2,1,0:T(8,128)(2,1)}), bf16[4,64,256]{2,1,0:T(8,128)(2,1)S(1)}, u32[]{:S(2)}, u32[]{:S(2)}) async-start(bf16[4,64,256]{2,1,0:T(8,128)(2,1)} %get-tuple-element.30.refs_2_), calls=%async_computation.2 | async-start | bytes 262144 | tf_op jit(solution)/shard_map/all_to_all | solution.py:414
  90.9 9.1 %collective-permute-start.12 = (bf16[512,3072]{1,0:T(8,128)(2,1)}, bf16[512,3072]{1,0:T(8,128)(2,1)S(1)}, u32[]{:S(2)}, u32[]{:S(2)}) collective-permute-start(bf16[512,3072]{1,0:T(8,128)(2,1)} %get-tuple-element.34), channel_id=1, source_target_pairs={{0,1},{1,0},{2,3},{3,2},{4,5},{5,4},{6,7},{7,6},{8,9},{9,8},{10,11... | collective-permute-start | bytes 9437192 | tf_op jit(solution)/shard_map/ppermute | solution.py:23
  91.0 20.3 %collective-permute-start.13 = (bf16[256,1024]{1,0:T(8,128)(2,1)}, bf16[256,1024]{1,0:T(8,128)(2,1)}, u32[]{:S(2)}, u32[]{:S(2)}) collective-permute-start(bf16[256,1024]{1,0:T(8,128)(2,1)} %get-tuple-element.38), channel_id=1, source_target_pairs={{0,8},{1,9},{2,10},{3,11},{4,12},{5,13},{6,14},{7,15},{8,0},{9,1},... | collective-permute-start | bytes 1572872 | tf_op jit(solution)/shard_map/ppermute | solution.py:23
  93.2 18.1 %collective-permute-start.15 = (bf16[256,1024]{1,0:T(8,128)(2,1)}, bf16[256,1024]{1,0:T(8,128)(2,1)}, u32[]{:S(2)}, u32[]{:S(2)}) collective-permute-start(bf16[256,1024]{1,0:T(8,128)(2,1)} %get-tuple-element.39), channel_id=1, source_target_pairs={{0,6},{1,7},{2,0},{3,1},{4,2},{5,3},{6,4},{7,5},{8,14},{9,15},{10,... | collective-permute-start | bytes 1572872 | tf_op jit(solution)/shard_map/ppermute | solution.py:23
  93.9 17.3 %collective-permute-start.14 = (bf16[256,1024]{1,0:T(8,128)(2,1)}, bf16[256,1024]{1,0:T(8,128)(2,1)}, u32[]{:S(2)}, u32[]{:S(2)}) collective-permute-start(bf16[256,1024]{1,0:T(8,128)(2,1)} %get-tuple-element.32.rest_0_), channel_id=1, source_target_pairs={{0,2},{1,3},{2,4},{3,5},{4,6},{5,7},{6,0},{7,1},{8,10},{9,11},{10,... | collective-permute-start | bytes 1572872 | tf_op jit(solution)/shard_map/ppermute | solution.py:23
  95.2 14.1 %all-to-all-start.3 = ((bf16[4,256,256]{2,1,0:T(8,128)(2,1)}), bf16[4,256,256]{2,1,0:T(8,128)(2,1)}, u32[]{:S(2)}, u32[]{:S(2)}) async-start(bf16[4,256,256]{2,1,0:T(8,128)(2,1)} %join_h.1.rest_8_), calls=%async_computation.3 | async-start | bytes 1048576 | tf_op jit(solution)/shard_map/all_to_all | solution.py:426
  100.0 1.6 %copy-start.2 = (bf16[512,3072]{1,0:T(8,128)(2,1)}, bf16[512,3072]{1,0:T(8,128)(2,1)S(1)}, u32[]{:S(2)}) copy-start(bf16[512,3072]{1,0:T(8,128)(2,1)S(1)} %collective-permute-done.12.a_ref) | copy-start | bytes 9437188
  (8 other events, 6.4 us)

commit v3 on v2

--- a/solution.py
+++ b/solution.py
@@ -42,55 +42,60 @@
 GRAD_DIMS = (((0,), (0,)), ((), ()))
 
 
+class Copies:
+    def __init__(self, sems):
+        self.sems, self.count = sems, 0
+
+    def __call__(self, src, dst):
+        c = pltpu.make_async_copy(src, dst, self.sems.at[self.count])
+        self.count += 1
+        c.start()
+        return c
+
+
+def wait_all(copies):
+    for c in copies:
+        c.wait()
+
+
 def far_gradients(here, tok, tok_rx, cot, cot_rx, after):
     rows, kv = cot.shape
-
-    def y_of(i, here):
-        step = jnp.where(i == 0, 2, jnp.where(i == 1, 1, jnp.where(i == 2, 3, 0)))
-        return (place(here[0])[1] + step) % NY
-
-    def own_block(i, here):
-        z, _, core = place(here[0])
-        return 0, block_at(1 - z, y_of(i, here), core)
-
-    def body(here_ref, t_ref, tr_ref, c_ref, cr_ref, *rest):
-        a_ref, b_ref, d_ref = rest[len(after) :]
-        i = pl.program_id(0)
-        acc = lax.dot_general(t_ref[...], c_ref[...], GRAD_DIMS, preferred_element_type=F32)
-        acc += lax.dot_general(tr_ref[...], cr_ref[...], GRAD_DIMS, preferred_element_type=F32)
-        acc = acc.astype(BF16)
-
-        @pl.when(i == 0)
-        def _():
-            a_ref[...] = acc
-
-        @pl.when((i == 1) | (i == 2))
-        def _():
-            b_ref[...] = acc
-
-        @pl.when(i == 3)
-        def _():
-            d_ref[...] = acc
+    deep = NY * 256
+
+    def body(here_ref, t_ref, tx_ref, c_ref, cx_ref, *rest):
+        a_ref, b_ref, d_ref, t_v, tx_v, c_v, cx_v, o_v, sems = rest[len(after) :]
+        z, y, core = place(here_ref[0])
+        copy = Copies(sems)
+        loads = [copy(c_ref, c_v), copy(cx_ref, cx_v)]
+        blocks = []
+        for k, step in enumerate((2, 1, NY - 1, 0)):
+            b = block_at(1 - z, (y + step) % NY, core)
+            blocks.append((copy(columns(t_ref, b), columns(t_v, k)), copy(columns(tx_ref, b), columns(tx_v, k))))
+        wait_all(loads)
+        targets = (a_ref, b_ref.at[pl.ds(0, 256)], b_ref.at[pl.ds(256, 256)], d_ref)
+        done = []
+        for k in range(NY):
+            wait_all(blocks[k])
+            at = slice(k * 256, k * 256 + 256)
+            acc = lax.dot_general(t_v[:, at], c_v[...], GRAD_DIMS, preferred_element_type=F32)
+            acc += lax.dot_general(tx_v[:, at], cx_v[...], GRAD_DIMS, preferred_element_type=F32)
+            o_v[at, :] = acc.astype(BF16)
+            done.append(copy(o_v.at[pl.ds(k * 256, 256)], targets[k]))
+        wait_all(done)
 
     return pl.pallas_call(
         body,
-        grid_spec=pltpu.PrefetchScalarGridSpec(
-            num_scalar_prefetch=1,
-            grid=(NY,),
-            in_specs=[
-                pl.BlockSpec((rows, 256), own_block),
-                pl.BlockSpec((rows, 256), own_block),
-                pl.BlockSpec((rows, kv), lambda i, here: (0, 0)),
-                pl.BlockSpec((rows, kv), lambda i, here: (0, 0)),
-            ]
-            + [ANY] * len(after),
-            out_specs=[
-                pl.BlockSpec((256, kv), lambda i, here: (0, 0)),
-                pl.BlockSpec((256, kv), lambda i, here: (jnp.clip(i - 1, 0, 1), 0)),
-                pl.BlockSpec((256, kv), lambda i, here: (0, 0)),
-            ],
-        ),
+        in_specs=[SMEM] + [ANY] * (4 + len(after)),
+        out_specs=[ANY] * 3,
         out_shape=[jax.ShapeDtypeStruct((m * 256, kv), BF16) for m in (1, 2, 1)],
+        scratch_shapes=[
+            pltpu.VMEM((rows, deep), BF16),
+            pltpu.VMEM((rows, deep), BF16),
+            pltpu.VMEM((rows, kv), BF16),
+            pltpu.VMEM((rows, kv), BF16),
+            pltpu.VMEM((deep, kv), BF16),
+            pltpu.SemaphoreType.DMA((3 * NY + 2,)),
+        ],
         compiler_params=pltpu.CompilerParams(vmem_limit_bytes=VMEM_LIMIT),
         name="far_gradients",
     )(here, tok, tok_rx, cot, cot_rx, *after)

time: 115 us -> 114 us (level)
  transfers between devices with their start and end apart: 20 -> 20, of which waited for: 5 -> 5; matrix products, arithmetic and copies ran while one was open for 2% -> 2% of each run, Pallas kernels for 32% -> 31%
where the time goes in v3:
time: 114 us; the launch traced here: 113 us
  Pallas kernels  49 us (43%)
  starting transfers between devices  43.5 us (38%)
  local copies, waits for them, and re-layouts  9.84 us (9%)
  waiting for transfers between devices  9.43 us (8%)
    pallas_call x2, Pallas kernels, project(): pl.pallas_call(body, in_specs=[SMEM] + [ANY] * (len(args) - 1), out_specs...  22.9 us
    ppermute x16, starting transfers between devices, shift_fsdp(): return lax.ppermute(a, 'fsdp', pairs)  18.6 us
    all_to_all x1, starting transfers between devices, on_device(): lax.all_to_all(synced, 'replica', 0, 0, axis_index_groups=H_GROUPS, tiled...  9.06 us
    pallas_call x3, Pallas kernels, add_blocks(): pl.pallas_call(body, grid=(1,), in_specs=[spec(k) for _, k, _ in flat] +...  8.23 us
    unnamed x24, local copies, waits for them, and re-layouts  7.73 us
    all_to_all x1, starting transfers between devices, on_device(): lax.all_to_all(parts, 'replica', 0, 0, axis_index_groups=H_GROUPS, tiled=...  6.72 us
    pallas_call x1, Pallas kernels, far_gradients(): pl.pallas_call(body, in_specs=[SMEM] + [ANY] * (4 + len(after)), out_spec...  6.17 us
    all_to_all x1, starting transfers between devices, on_device(): lax.all_to_all(ready, 'replica', 0, 0, axis_index_groups=X_GROUPS, tiled=...  4.79 us
  transfers between devices with their start and end apart: 20, of which 5 were waited for; matrix products, arithmetic and copies ran while one was open for 2% of the time, Pallas kernels for 31%

profile of v3, /device:TPU:32, one launch (start us, length us, event | category | flops | bytes accessed | tf_op | source)
XLA Modules:
  0.0 113.1 jit_solution(17321894513135111981)
XLA Ops:
  1.2 1.6 %collective-permute-start.6 = (bf16[256,1024]{1,0:T(8,128)(2,1)}, bf16[256,1024]{1,0:T(8,128)(2,1)S(1)}, u32[]{:S(2)}, u32[]{:S(2)}) collective-permute-start(bf16[256,1024]{1,0:T(8,128)(2,1)} %bitcast.27), channel_id=1, source_target_pairs={{0,2},{1,3},{2,4},{3,5},{4,6},{5,7},{6,0},{7,1},{8,10},{9,11},{10,... | collective-permute-start | bytes 1572872 | tf_op jit(solution)/shard_map/ppermute | solution.py:23
  3.1 3.2 %collective-permute-start.7 = (bf16[256,1024]{1,0:T(8,128)(2,1)}, bf16[256,1024]{1,0:T(8,128)(2,1)S(1)}, u32[]{:S(2)}, u32[]{:S(2)}) collective-permute-start(bf16[256,1024]{1,0:T(8,128)(2,1)} %bitcast.29), channel_id=1, source_target_pairs={{0,6},{1,7},{2,0},{3,1},{4,2},{5,3},{6,4},{7,5},{8,14},{9,15},{10,... | collective-permute-start | bytes 1572872 | tf_op jit(solution)/shard_map/ppermute | solution.py:23
  8.4 6.7 %all-to-all-start = ((bf16[4,256,256]{2,1,0:T(8,128)(2,1)}), bf16[4,256,256]{2,1,0:T(8,128)(2,1)}, u32[]{:S(2)}, u32[]{:S(2)}) async-start(bf16[4,256,256]{2,1,0:T(8,128)(2,1)} %bitcast.8), calls=%async_computation | async-start | bytes 1048576 | tf_op jit(solution)/shard_map/all_to_all | solution.py:395
  17.6 2.9 %collective-permute-start.4 = (bf16[256,1024]{1,0:T(8,128)(2,1)}, bf16[256,1024]{1,0:T(8,128)(2,1)S(1)}, u32[]{:S(2)}, u32[]{:S(2)}) collective-permute-start(bf16[256,1024]{1,0:T(8,128)(2,1)} %collective-permute-done.2.rest_0_), channel_id=1, source_target_pairs={{0,6},{1,7},{2,0},{3,1},{4,2},{5,3},{6,4},{7,5},{8,14},{9,15},{10,... | collective-permute-start | bytes 1572872 | tf_op jit(solution)/shard_map/ppermute | solution.py:23
  21.7 6.2 %far_gradients.1 = (bf16[256,1024]{1,0:T(8,128)(2,1)}, bf16[512,1024]{1,0:T(8,128)(2,1)}, bf16[256,1024]{1,0:T(8,128)(2,1)}) custom-call(s32[2]{0:T(128)} %pad_add_fusion.here_ref, bf16[512,4096]{1,0:T(8,128)(2,1)} %bitcast.19, bf16[512,4096]{1,0:T(8,128)(2,1)} %collective-permute-done.tx_ref, bf16[512,1024]{1,0:T(8,128)(2,1)} %bitcast.24, ...), custom_call_target="tpu_custom_call" | custom-call | tf_op jit(solution)/shard_map/far_gradients/pallas_call | solution.py:86
  27.9 1.9 %collective-permute-start.10 = (bf16[256,1024]{1,0:T(8,128)(2,1)}, bf16[256,1024]{1,0:T(8,128)(2,1)S(1)}, u32[]{:S(2)}, u32[]{:S(2)}) collective-permute-start(bf16[256,1024]{1,0:T(8,128)(2,1)} %get-tuple-element.24.rest_0_), channel_id=1, source_target_pairs={{0,8},{1,9},{2,10},{3,11},{4,12},{5,13},{6,14},{7,15},{8,0},{9,1},... | collective-permute-start | bytes 1572872 | tf_op jit(solution)/shard_map/ppermute | solution.py:23
  31.0 1.8 %sum_along_h.1.rest_4_ = bf16[4,64,256]{2,1,0:T(8,128)(2,1)} custom-call(s32[2]{0:T(128)} %pad_add_fusion.here_ref, bf16[4,256,256]{2,1,0:T(8,128)(2,1)} %all-to-all-done.p_ref, bf16[256,1024]{1,0:T(8,128)(2,1)} %get-tuple-element.24.rest_0_), custom_call_target="tpu_custom_call" | custom-call | tf_op jit(solution)/shard_map/sum_along_h/pallas_call | solution.py:335
  32.8 4.3 %all-to-all-start.1 = ((bf16[4,64,256]{2,1,0:T(8,128)(2,1)}), bf16[4,64,256]{2,1,0:T(8,128)(2,1)S(1)}, u32[]{:S(2)}, u32[]{:S(2)}) async-start(bf16[4,64,256]{2,1,0:T(8,128)(2,1)} %sum_along_h.1.rest_4_), calls=%async_computation.1 | async-start | bytes 262144 | tf_op jit(solution)/shard_map/all_to_all | solution.py:408
  37.1 12.2 %project.2 = (f32[512,1024]{1,0:T(8,128)}, bf16[512,4096]{1,0:T(8,128)(2,1)}, bf16[512,3072]{1,0:T(8,128)(2,1)}, f32[512,1024]{1,0:T(8,128)}, f32[1024,1024]{1,0:T(8,128)}) custom-call(s32[2]{0:T(128)} %pad_add_fusion.here_ref, bf16[512,4096]{1,0:T(8,128)(2,1)} %bitcast.20, bf16[512,4096]{1,0:T(8,128)(2,1)} %collective-permute-done.tx_ref, ...), custom_call_target="tpu_custom_call" | custom-call | tf_op jit(solution)/shard_map/project/pallas_call | solution.py:242
  50.0 1.7 %outer_step.1 = (f32[64,256]{1,0:T(8,128)}, f32[64,256]{1,0:T(8,128)}, bf16[4,64,256]{2,1,0:T(8,128)(2,1)}) custom-call(s32[2]{0:T(128)} %pad_add_fusion.here_ref, bf16[4,64,256]{2,1,0:T(8,128)(2,1)} %copy-done.9, f32[64,256]{1,0:T(8,128)} %bitcast.35, f32[64,256]{1,0:T(8,128)} %bitcast.36, f32[1024,1024]{1,0:T(8,128)} %get-tuple-element.29.rest_0_.refs_0_.refs_1_), custom_call_target="tpu_custom_call" | custom-call | tf_op jit(solution)/shard_map/outer_step/pallas_call | solution.py:354
  52.8 2.2 %add_blocks.3 = bf16[256,1024]{1,0:T(8,128)(2,1)} custom-call(f32[1024,1024]{1,0:T(8,128)} %get-tuple-element.29.rest_0_.refs_0_.refs_1_, bf16[256,1024]{1,0:T(8,128)(2,1)} %copy-done.7, bf16[4,64,256]{2,1,0:T(8,128)(2,1)} %get-tuple-element.30.refs_2_, bf16[256,1024]{1,0:T(8,128)(2,1)} %copy-done.4, bf16[256,1024]{1,0:T(8,128)(2,1)} %copy-done.3), custom_call_target="tpu_custom_call" | custom-call | tf_op jit(solution)/shard_map/add_blocks/pallas_call | solution.py:122
  56.3 2.0 %collective-permute-start.5 = (bf16[256,1024]{1,0:T(8,128)(2,1)}, bf16[256,1024]{1,0:T(8,128)(2,1)S(1)}, u32[]{:S(2)}, u32[]{:S(2)}) collective-permute-start(bf16[256,1024]{1,0:T(8,128)(2,1)} %copy-done.3), channel_id=1, source_target_pairs={{0,6},{1,7},{2,0},{3,1},{4,2},{5,3},{6,4},{7,5},{8,14},{9,15},{10,... | collective-permute-start | bytes 1572872 | tf_op jit(solution)/shard_map/ppermute | solution.py:23
  58.2 9.1 %all-to-all-start.2 = ((bf16[4,64,256]{2,1,0:T(8,128)(2,1)}), bf16[4,64,256]{2,1,0:T(8,128)(2,1)S(1)}, u32[]{:S(2)}, u32[]{:S(2)}) async-start(bf16[4,64,256]{2,1,0:T(8,128)(2,1)} %get-tuple-element.30.refs_2_), calls=%async_computation.2 | async-start | bytes 262144 | tf_op jit(solution)/shard_map/all_to_all | solution.py:419
  70.2 3.1 %add_blocks.4 = (bf16[256,1024]{1,0:T(8,128)(2,1)}, bf16[256,1024]{1,0:T(8,128)(2,1)}) custom-call(f32[1024,1024]{1,0:T(8,128)} %get-tuple-element.29.rest_0_.refs_0_.refs_1_, f32[1024,1024]{1,0:T(8,128)} %get-tuple-element.29.rest_0_.refs_0_.refs_1_, bf16[512,1024]{1,0:T(8,128)(2,1)} %copy-done.1, bf16[256,1024]{1,0:T(8,128)(2,1)} %copy-done.11, ...), custom_call_target="tpu_custom_call" | custom-call | tf_op jit(solution)/shard_map/add_blocks/pallas_call | solution.py:122
  73.3 2.5 %all-to-all-done.2.p_ref = bf16[4,64,256]{2,1,0:T(8,128)(2,1)S(1)} async-done(((bf16[4,64,256]{2,1,0:T(8,128)(2,1)}), bf16[4,64,256]{2,1,0:T(8,128)(2,1)S(1)}, u32[]{:S(2)}, u32[]{:S(2)}) %all-to-all-start.2) | async-done | bytes 131104 | tf_op jit(solution)/shard_map/all_to_all | solution.py:419
  76.5 1.8 %join_h.1.rest_8_ = bf16[4,256,256]{2,1,0:T(8,128)(2,1)} custom-call(s32[2]{0:T(128)} %pad_add_fusion.here_ref, bf16[4,64,256]{2,1,0:T(8,128)(2,1)} %copy-done.10, bf16[256,1024]{1,0:T(8,128)(2,1)} %get-tuple-element.32.rest_0_), custom_call_target="tpu_custom_call" | custom-call | tf_op jit(solution)/shard_map/join_h/pallas_call | solution.py:366
  79.1 10.7 %project.3 = (f32[512,1024]{1,0:T(8,128)}, bf16[512,4096]{1,0:T(8,128)(2,1)}, bf16[512,3072]{1,0:T(8,128)(2,1)}) custom-call(s32[2]{0:T(128)} %pad_add_fusion.here_ref, bf16[512,4096]{1,0:T(8,128)(2,1)} %bitcast.21, bf16[512,4096]{1,0:T(8,128)(2,1)} %collective-permute-done.tx_ref, ...), custom_call_target="tpu_custom_call", output_to_operand_aliasing={{1}: (11, {}), {2}: (12, {})} | custom-call | tf_op jit(solution)/shard_map/project/pallas_call | solution.py:242
  90.0 2.2 %collective-permute-start.13 = (bf16[256,1024]{1,0:T(8,128)(2,1)}, bf16[256,1024]{1,0:T(8,128)(2,1)}, u32[]{:S(2)}, u32[]{:S(2)}) collective-permute-start(bf16[256,1024]{1,0:T(8,128)(2,1)} %get-tuple-element.38), channel_id=1, source_target_pairs={{0,8},{1,9},{2,10},{3,11},{4,12},{5,13},{6,14},{7,15},{8,0},{9,1},... | collective-permute-start | bytes 1572872 | tf_op jit(solution)/shard_map/ppermute | solution.py:23
  94.2 4.8 %all-to-all-start.3 = ((bf16[4,256,256]{2,1,0:T(8,128)(2,1)}), bf16[4,256,256]{2,1,0:T(8,128)(2,1)}, u32[]{:S(2)}, u32[]{:S(2)}) async-start(bf16[4,256,256]{2,1,0:T(8,128)(2,1)} %join_h.1.rest_8_), calls=%async_computation.3 | async-start | bytes 1048576 | tf_op jit(solution)/shard_map/all_to_all | solution.py:431
  99.0 1.6 %copy-done.2 = bf16[512,3072]{1,0:T(8,128)(2,1)} copy-done((bf16[512,3072]{1,0:T(8,128)(2,1)}, bf16[512,3072]{1,0:T(8,128)(2,1)S(1)}, u32[]{:S(2)}) %copy-start.2) | copy-done | bytes 3145752
  100.7 4.5 %merge.1 = (bf16[512,1024]{1,0:T(8,128)(2,1)}, bf16[512,4096]{1,0:T(8,128)(2,1)}) custom-call(s32[2]{0:T(128)} %pad_add_fusion.here_ref, f32[512,1024]{1,0:T(8,128)} %get-tuple-element.33.own_ref.rest_0_, bf16[512,3072]{1,0:T(8,128)(2,1)} %copy-done.2, bf16[512,4096]{1,0:T(8,128)(2,1)} %get-tuple-element.35._, ...), custom_call_target="tpu_custom_call", output_to_operand_aliasing={{1}: (3, {})} | custom-call | tf_op jit(solution)/shard_map/merge/pallas_call | solution.py:285
  105.1 3.2 %all-to-all-done.3.p_ref = bf16[4,256,256]{2,1,0:T(8,128)(2,1)} async-done(((bf16[4,256,256]{2,1,0:T(8,128)(2,1)}), bf16[4,256,256]{2,1,0:T(8,128)(2,1)}, u32[]{:S(2)}, u32[]{:S(2)}) %all-to-all-start.3) | async-done | bytes 524320 | tf_op jit(solution)/shard_map/all_to_all | solution.py:431
  108.4 1.9 %join_x.1.refs_4_ = bf16[256,1024]{1,0:T(8,128)(2,1)} custom-call(s32[2]{0:T(128)} %pad_add_fusion.here_ref, bf16[4,256,256]{2,1,0:T(8,128)(2,1)} %all-to-all-done.3.p_ref, bf16[512,1024]{1,0:T(8,128)(2,1)} %get-tuple-element.36.rest_0_), custom_call_target="tpu_custom_call" | custom-call | tf_op jit(solution)/shard_map/join_x/pallas_call | solution.py:378
  110.3 2.9 %add_blocks.5 = f32[256,1024]{1,0:T(8,128)} custom-call(f32[1024,1024]{1,0:T(8,128)} %get-tuple-element.29.rest_0_.refs_0_.refs_1_, bf16[256,1024]{1,0:T(8,128)(2,1)} %collective-permute-done.13.refs_1_, bf16[256,1024]{1,0:T(8,128)(2,1)} %collective-permute-done.14.refs_2_, bf16[256,1024]{1,0:T(8,128)(2,1)} %collective-permute-done.15.refs_3_, ...), custom_call_target="tpu_custom_call" | custom-call | tf_op jit(solution)/shard_map/add_blocks/pallas_call | solution.py:122
  (54 shorter events, 17.3 us)
Async XLA Ops:
  0.6 19.9 %collective-permute-start = (bf16[512,4096]{1,0:T(8,128)(2,1)}, bf16[512,4096]{1,0:T(8,128)(2,1)}, u32[]{:S(2)}, u32[]{:S(2)}) collective-permute-start(bf16[512,4096]{1,0:T(8,128)(2,1)} %bitcast.18), channel_id=1, source_target_pairs={{0,1},{1,0},{2,3},{3,2},{4,5},{5,4},{6,7},{7,6},{8,9},{9,8},{10,11... | collective-permute-start | bytes 12582920 | tf_op jit(solution)/shard_map/ppermute | solution.py:23
  0.7 19.8 %collective-permute-start.1 = (bf16[512,1024]{1,0:T(8,128)(2,1)}, bf16[512,1024]{1,0:T(8,128)(2,1)S(1)}, u32[]{:S(2)}, u32[]{:S(2)}) collective-permute-start(bf16[512,1024]{1,0:T(8,128)(2,1)} %bitcast.23), channel_id=1, source_target_pairs={{0,1},{1,0},{2,3},{3,2},{4,5},{5,4},{6,7},{7,6},{8,9},{9,8},{10,11... | collective-permute-start | bytes 3145736 | tf_op jit(solution)/shard_map/ppermute | solution.py:23
  1.2 15.4 %collective-permute-start.6 = (bf16[256,1024]{1,0:T(8,128)(2,1)}, bf16[256,1024]{1,0:T(8,128)(2,1)S(1)}, u32[]{:S(2)}, u32[]{:S(2)}) collective-permute-start(bf16[256,1024]{1,0:T(8,128)(2,1)} %bitcast.27), channel_id=1, source_target_pairs={{0,2},{1,3},{2,4},{3,5},{4,6},{5,7},{6,0},{7,1},{8,10},{9,11},{10,... | collective-permute-start | bytes 1572872 | tf_op jit(solution)/shard_map/ppermute | solution.py:23
  2.8 14.8 %collective-permute-start.2 = (bf16[256,1024]{1,0:T(8,128)(2,1)}, bf16[256,1024]{1,0:T(8,128)(2,1)}, u32[]{:S(2)}, u32[]{:S(2)}) collective-permute-start(bf16[256,1024]{1,0:T(8,128)(2,1)} %bitcast.28), channel_id=1, source_target_pairs={{0,8},{1,9},{2,10},{3,11},{4,12},{5,13},{6,14},{7,15},{8,0},{9,1},... | collective-permute-start | bytes 1572872 | tf_op jit(solution)/shard_map/ppermute | solution.py:23
  3.1 17.5 %collective-permute-start.7 = (bf16[256,1024]{1,0:T(8,128)(2,1)}, bf16[256,1024]{1,0:T(8,128)(2,1)S(1)}, u32[]{:S(2)}, u32[]{:S(2)}) collective-permute-start(bf16[256,1024]{1,0:T(8,128)(2,1)} %bitcast.29), channel_id=1, source_target_pairs={{0,6},{1,7},{2,0},{3,1},{4,2},{5,3},{6,4},{7,5},{8,14},{9,15},{10,... | collective-permute-start | bytes 1572872 | tf_op jit(solution)/shard_map/ppermute | solution.py:23
  8.4 22.6 %all-to-all-start = ((bf16[4,256,256]{2,1,0:T(8,128)(2,1)}), bf16[4,256,256]{2,1,0:T(8,128)(2,1)}, u32[]{:S(2)}, u32[]{:S(2)}) async-start(bf16[4,256,256]{2,1,0:T(8,128)(2,1)} %bitcast.8), calls=%async_computation | async-start | bytes 1048576 | tf_op jit(solution)/shard_map/all_to_all | solution.py:395
  16.6 3.9 %copy-start.5 = (bf16[256,1024]{1,0:T(8,128)(2,1)}, bf16[256,1024]{1,0:T(8,128)(2,1)S(1)}, u32[]{:S(2)}) copy-start(bf16[256,1024]{1,0:T(8,128)(2,1)S(1)} %collective-permute-done.6.rest_0_.rest_1_) | copy-start | bytes 1572868
  16.6 20.5 %collective-permute-start.8 = (bf16[256,1024]{1,0:T(8,128)(2,1)S(1)}, bf16[256,1024]{1,0:T(8,128)(2,1)}, u32[]{:S(2)}, u32[]{:S(2)}) collective-permute-start(bf16[256,1024]{1,0:T(8,128)(2,1)S(1)} %collective-permute-done.6.rest_0_.rest_1_), channel_id=1, source_target_pairs={{0,2},{1,3},{2,4},{3,5},{4,6},{5,7},{6,0},{7,1},{8,10},{9,11},{10,... | collective-permute-start | bytes 1572872 | tf_op jit(solution)/shard_map/ppermute | solution.py:23
  17.6 34.0 %collective-permute-start.4 = (bf16[256,1024]{1,0:T(8,128)(2,1)}, bf16[256,1024]{1,0:T(8,128)(2,1)S(1)}, u32[]{:S(2)}, u32[]{:S(2)}) collective-permute-start(bf16[256,1024]{1,0:T(8,128)(2,1)} %collective-permute-done.2.rest_0_), channel_id=1, source_target_pairs={{0,6},{1,7},{2,0},{3,1},{4,2},{5,3},{6,4},{7,5},{8,14},{9,15},{10,... | collective-permute-start | bytes 1572872 | tf_op jit(solution)/shard_map/ppermute | solution.py:23
  20.5 31.1 %collective-permute-start.3 = (bf16[256,1024]{1,0:T(8,128)(2,1)}, bf16[256,1024]{1,0:T(8,128)(2,1)S(1)}, u32[]{:S(2)}, u32[]{:S(2)}) collective-permute-start(bf16[256,1024]{1,0:T(8,128)(2,1)} %collective-permute-done.2.rest_0_), channel_id=1, source_target_pairs={{0,2},{1,3},{2,4},{3,5},{4,6},{5,7},{6,0},{7,1},{8,10},{9,11},{10,... | collective-permute-start | bytes 1572872 | tf_op jit(solution)/shard_map/ppermute | solution.py:23
  20.6 1.1 copy-start
  27.9 23.8 %collective-permute-start.10 = (bf16[256,1024]{1,0:T(8,128)(2,1)}, bf16[256,1024]{1,0:T(8,128)(2,1)S(1)}, u32[]{:S(2)}, u32[]{:S(2)}) collective-permute-start(bf16[256,1024]{1,0:T(8,128)(2,1)} %get-tuple-element.24.rest_0_), channel_id=1, source_target_pairs={{0,8},{1,9},{2,10},{3,11},{4,12},{5,13},{6,14},{7,15},{8,0},{9,1},... | collective-permute-start | bytes 1572872 | tf_op jit(solution)/shard_map/ppermute | solution.py:23
  29.7 38.7 %collective-permute-start.9 = (bf16[512,1024]{1,0:T(8,128)(2,1)}, bf16[512,1024]{1,0:T(8,128)(2,1)S(1)}, u32[]{:S(2)}, u32[]{:S(2)}) collective-permute-start(bf16[512,1024]{1,0:T(8,128)(2,1)} %get-tuple-element.31), channel_id=1, source_target_pairs={{0,8},{1,9},{2,10},{3,11},{4,12},{5,13},{6,14},{7,15},{8,0},{9,1},... | collective-permute-start | bytes 3145736 | tf_op jit(solution)/shard_map/ppermute | solution.py:23
  32.8 16.5 %all-to-all-start.1 = ((bf16[4,64,256]{2,1,0:T(8,128)(2,1)}), bf16[4,64,256]{2,1,0:T(8,128)(2,1)S(1)}, u32[]{:S(2)}, u32[]{:S(2)}) async-start(bf16[4,64,256]{2,1,0:T(8,128)(2,1)} %sum_along_h.1.rest_4_), calls=%async_computation.1 | async-start | bytes 262144 | tf_op jit(solution)/shard_map/all_to_all | solution.py:408
  51.7 1.1 copy-start.7
  55.0 13.4 %collective-permute-start.11 = (bf16[256,1024]{1,0:T(8,128)(2,1)}, bf16[256,1024]{1,0:T(8,128)(2,1)S(1)}, u32[]{:S(2)}, u32[]{:S(2)}) collective-permute-start(bf16[256,1024]{1,0:T(8,128)(2,1)} %add_blocks.3), channel_id=1, source_target_pairs={{0,2},{1,3},{2,4},{3,5},{4,6},{5,7},{6,0},{7,1},{8,10},{9,11},{10,... | collective-permute-start | bytes 1572872 | tf_op jit(solution)/shard_map/ppermute | solution.py:23
  56.3 22.1 %collective-permute-start.5 = (bf16[256,1024]{1,0:T(8,128)(2,1)}, bf16[256,1024]{1,0:T(8,128)(2,1)S(1)}, u32[]{:S(2)}, u32[]{:S(2)}) collective-permute-start(bf16[256,1024]{1,0:T(8,128)(2,1)} %copy-done.3), channel_id=1, source_target_pairs={{0,6},{1,7},{2,0},{3,1},{4,2},{5,3},{6,4},{7,5},{8,14},{9,15},{10,... | collective-permute-start | bytes 1572872 | tf_op jit(solution)/shard_map/ppermute | solution.py:23
  58.2 17.6 %all-to-all-start.2 = ((bf16[4,64,256]{2,1,0:T(8,128)(2,1)}), bf16[4,64,256]{2,1,0:T(8,128)(2,1)S(1)}, u32[]{:S(2)}, u32[]{:S(2)}) async-start(bf16[4,64,256]{2,1,0:T(8,128)(2,1)} %get-tuple-element.30.refs_2_), calls=%async_computation.2 | async-start | bytes 262144 | tf_op jit(solution)/shard_map/all_to_all | solution.py:419
  89.9 9.1 %collective-permute-start.12 = (bf16[512,3072]{1,0:T(8,128)(2,1)}, bf16[512,3072]{1,0:T(8,128)(2,1)S(1)}, u32[]{:S(2)}, u32[]{:S(2)}) collective-permute-start(bf16[512,3072]{1,0:T(8,128)(2,1)} %get-tuple-element.34), channel_id=1, source_target_pairs={{0,1},{1,0},{2,3},{3,2},{4,5},{5,4},{6,7},{7,6},{8,9},{9,8},{10,11... | collective-permute-start | bytes 9437192 | tf_op jit(solution)/shard_map/ppermute | solution.py:23
  90.0 20.3 %collective-permute-start.13 = (bf16[256,1024]{1,0:T(8,128)(2,1)}, bf16[256,1024]{1,0:T(8,128)(2,1)}, u32[]{:S(2)}, u32[]{:S(2)}) collective-permute-start(bf16[256,1024]{1,0:T(8,128)(2,1)} %get-tuple-element.38), channel_id=1, source_target_pairs={{0,8},{1,9},{2,10},{3,11},{4,12},{5,13},{6,14},{7,15},{8,0},{9,1},... | collective-permute-start | bytes 1572872 | tf_op jit(solution)/shard_map/ppermute | solution.py:23
  92.2 18.1 %collective-permute-start.15 = (bf16[256,1024]{1,0:T(8,128)(2,1)}, bf16[256,1024]{1,0:T(8,128)(2,1)}, u32[]{:S(2)}, u32[]{:S(2)}) collective-permute-start(bf16[256,1024]{1,0:T(8,128)(2,1)} %get-tuple-element.39), channel_id=1, source_target_pairs={{0,6},{1,7},{2,0},{3,1},{4,2},{5,3},{6,4},{7,5},{8,14},{9,15},{10,... | collective-permute-start | bytes 1572872 | tf_op jit(solution)/shard_map/ppermute | solution.py:23
  93.0 17.3 %collective-permute-start.14 = (bf16[256,1024]{1,0:T(8,128)(2,1)}, bf16[256,1024]{1,0:T(8,128)(2,1)}, u32[]{:S(2)}, u32[]{:S(2)}) collective-permute-start(bf16[256,1024]{1,0:T(8,128)(2,1)} %get-tuple-element.32.rest_0_), channel_id=1, source_target_pairs={{0,2},{1,3},{2,4},{3,5},{4,6},{5,7},{6,0},{7,1},{8,10},{9,11},{10,... | collective-permute-start | bytes 1572872 | tf_op jit(solution)/shard_map/ppermute | solution.py:23
  94.2 14.1 %all-to-all-start.3 = ((bf16[4,256,256]{2,1,0:T(8,128)(2,1)}), bf16[4,256,256]{2,1,0:T(8,128)(2,1)}, u32[]{:S(2)}, u32[]{:S(2)}) async-start(bf16[4,256,256]{2,1,0:T(8,128)(2,1)} %join_h.1.rest_8_), calls=%async_computation.3 | async-start | bytes 1048576 | tf_op jit(solution)/shard_map/all_to_all | solution.py:431
  99.0 1.6 %copy-start.2 = (bf16[512,3072]{1,0:T(8,128)(2,1)}, bf16[512,3072]{1,0:T(8,128)(2,1)S(1)}, u32[]{:S(2)}) copy-start(bf16[512,3072]{1,0:T(8,128)(2,1)S(1)} %collective-permute-done.12.a_ref) | copy-start | bytes 9437188
  (8 other events, 6.4 us)
